TPU v7x, 256 devices: a whole 4x4x8 slice. The times are simulated.
256 devices in a mesh: gx: 16 (over z, core), gy: 4 (over x), gz: 4 (over y).
Axes of the slice: x: 4, y: 4, z: 8, core: 2. Of those that a mesh axis runs over, the one named last changes fastest.
Arguments:
- sim_density: float32 [128, 8, 128, 512], P('gx', None, 'gy', 'gz'), may hold values from 0.002 to 3, as said below
- brick_home: int32 [128, 4, 4], P('gx', 'gy', 'gz'), may hold values from 0 to 127, as said below
- jitter: int32 [1024, 128], P('gx', 'gy'), may hold values from 0 to 15
Outputs:
- image: float32 [2, 256, 32], P(None, 'gx', ('gy', 'gz'))
Inputs may be any that keep to these rules, and one draw needn't show every extreme that they name: `brick_home`: within each group of equal second and third indices the entries are a permutation; entry h places the brick on the gx device h // 8 at slot h % 8. That device lies at most 2 positions away along gx, counted cyclically; no device sends more than 2 bricks to one device (itself included), some device of every group sends exactly 2, and all devices of a group send equally many bricks to the device a given number of positions further. `sim_density`: a positive density.
All inputs are finite; a program needn't handle non-finite values.
Results may differ from a plain program's by a relative error of at most 0.0001.
Values sent between devices are 32-bit elements; how exact they have to be, the bound alone decides.
No kernel may reach another device: no remote copies, remote signals or barrier semaphores. Data moves between devices by JAX's collectives and lax.ppermute only.
A program may use at most 64 MiB of HBM per device.

v0:
```python
import jax
import jax.numpy as jnp
from jax import lax
from jax.sharding import PartitionSpec as P

STRIDE = 16
MT = 8
PIXEL = 4
REACH = 2


GLOW = 5.0
DEPTH_GAIN = 12.0


def shifted(value, axis, steps):
    count = lax.axis_size(axis)
    pairs = [(source, (source + steps) % count) for source in range(count)]
    return lax.ppermute(value, axis, pairs)


def owner_rank(owners):
    places = jnp.arange(owners.shape[0])
    same_owner = owners[:, None] == owners[None, :]
    earlier = places[None, :] < places[:, None]
    return jnp.sum(same_owner & earlier, axis=1)


def place_rows(values, targets, total_rows):
    empty_rows = jnp.zeros((total_rows,) + values.shape[1:], values.dtype)
    return empty_rows.at[targets].set(values, mode="drop")


def label_rows(labels, targets, total_rows, empty_label):
    empty_rows = jnp.full((total_rows,), empty_label, jnp.int32)
    return empty_rows.at[targets].set(labels, mode="drop")


def tile_peaks(bricks):
    brick_total, brick_rows, brick_cols, brick_depth = bricks.shape
    depth_peak = bricks.max(axis=3)
    shaped = depth_peak.reshape(brick_total, brick_rows // MT, MT, brick_cols // MT, MT)
    return shaped.max(axis=(2, 4))


def share_peaks(peak_tiles):
    return lax.pmax(peak_tiles, "gz")


def pool_pixels(field):
    return field.reshape(field.shape[0] // PIXEL, PIXEL, field.shape[1] // PIXEL, PIXEL).mean(
        axis=(1, 3)
    )


def render(bricks, peak_tiles, offsets, absorb):
    brick_total, brick_rows, brick_cols, brick_depth = bricks.shape
    columns = brick_total * brick_rows * brick_cols
    collide = brick_depth // STRIDE
    majorant = jnp.repeat(jnp.repeat(peak_tiles, MT, axis=1), MT, axis=2).reshape(1, columns)
    cell_rows = bricks.reshape(columns, brick_depth)
    depth_place = lax.broadcasted_iota(jnp.int32, (1, brick_depth), 1)
    chosen = depth_place % STRIDE == offsets.reshape(columns, 1)
    masked = jnp.where(chosen, cell_rows, jnp.float32(0.0))
    picker_rows = lax.broadcasted_iota(jnp.int32, (collide, brick_depth), 0)
    picker_cols = lax.broadcasted_iota(jnp.int32, (collide, brick_depth), 1)
    picker = (picker_cols // STRIDE == picker_rows).astype(jnp.float32)
    samples = lax.dot_general(
        picker,
        masked,
        (((1,), (1,)), ((), ())),
        precision=lax.Precision.HIGHEST,
        preferred_element_type=jnp.float32,
    )
    ratios = absorb * samples / majorant
    keeping = 1.0 - ratios
    through = jnp.cumprod(keeping, axis=0)
    shading = jnp.concatenate([jnp.ones_like(keeping[:1]), through[:-1]], axis=0)
    radiance = jnp.sum(shading * ratios * (GLOW * samples), axis=0)
    shape_out = (brick_total, brick_rows, brick_cols)
    return (radiance.reshape(shape_out), through[-1].reshape(shape_out))


def shards(sim_density, brick_home, jitter):
    brick_total = sim_density.shape[0]
    brick_rows = sim_density.shape[1]
    brick_cols = sim_density.shape[2]
    brick_depth = sim_density.shape[3]
    groups_x = lax.axis_size("gx")
    layers_z = lax.axis_size("gz")
    spread = min(2 * REACH + 1, groups_x)
    capacity = (brick_total + spread - 1) // spread
    absorb = DEPTH_GAIN / (brick_depth // STRIDE * layers_z)
    home_index = brick_home.reshape(brick_total)
    owners = home_index // brick_total
    home_slot = home_index % brick_total
    before = owner_rank(owners)
    offsets_home = jitter.reshape(brick_total, brick_rows, brick_cols)
    position = lax.axis_index("gx")
    chosen_shifts = []
    for shift_by in sorted(range(-REACH, REACH + 1), key=abs):
        chosen_shifts.append(shift_by)
    wanted_list = []
    slot_list = []
    for shift_by in chosen_shifts:
        wanted = owners == (position + shift_by) % groups_x
        wanted_list.append(wanted)
        slot_list.append(jnp.where(wanted, before, capacity))
    own_peaks = tile_peaks(sim_density)
    arrived_peaks = []
    arrived_labels = []
    for section, shift_by in enumerate(chosen_shifts):
        packed = place_rows(own_peaks, slot_list[section], capacity)
        packed_labels = label_rows(home_slot, slot_list[section], capacity, brick_total)
        if shift_by == 0:
            arrived = (packed, packed_labels)
        else:
            arrived = shifted((packed, packed_labels), "gx", shift_by)
        arrived_peaks.append(arrived[0])
        arrived_labels.append(arrived[1])
    home_peaks = share_peaks(
        place_rows(
            jnp.concatenate(arrived_peaks, axis=0),
            jnp.concatenate(arrived_labels, axis=0),
            brick_total,
        )
    )
    mine_peaks = jnp.zeros_like(own_peaks)
    mine_offsets = jnp.zeros_like(offsets_home)
    picked_rows = jnp.minimum(before, capacity - 1)
    for section, shift_by in enumerate(chosen_shifts):
        lookup = jnp.minimum(arrived_labels[section], brick_total - 1)
        reply = (home_peaks[lookup], offsets_home[lookup])
        if shift_by == 0:
            returned = reply
        else:
            returned = shifted((reply[0], reply[1]), "gx", -shift_by)
        wanted = wanted_list[section]
        mine_peaks = jnp.where(wanted[:, None, None], returned[0][picked_rows], mine_peaks)
        mine_offsets = jnp.where(wanted[:, None, None], returned[1][picked_rows], mine_offsets)
    own_radiance, own_transmit = render(sim_density, mine_peaks, mine_offsets, absorb)
    got_radiance = []
    got_transmit = []
    for section, shift_by in enumerate(chosen_shifts):
        packed_radiance = place_rows(own_radiance, slot_list[section], capacity)
        packed_transmit = place_rows(own_transmit, slot_list[section], capacity)
        if shift_by == 0:
            arrived = (packed_radiance, packed_transmit)
        else:
            arrived = shifted((packed_radiance, packed_transmit), "gx", shift_by)
        got_radiance.append(arrived[0])
        got_transmit.append(arrived[1])
    all_labels = jnp.concatenate(arrived_labels, axis=0)
    radiance = place_rows(jnp.concatenate(got_radiance, axis=0), all_labels, brick_total)
    transmit = place_rows(jnp.concatenate(got_transmit, axis=0), all_labels, brick_total)
    column_radiance = radiance.reshape(1, brick_total * brick_rows, brick_cols)
    column_transmit = transmit.reshape(1, brick_total * brick_rows, brick_cols)
    depth_radiance, depth_transmit = (
        lax.all_to_all(column_radiance, "gz", split_axis=2, concat_axis=0, tiled=True),
        lax.all_to_all(column_transmit, "gz", split_axis=2, concat_axis=0, tiled=True),
    )
    through = jnp.cumprod(depth_transmit, axis=0)
    shading = jnp.concatenate([jnp.ones_like(depth_transmit[:1]), through[:-1]], axis=0)
    total_radiance = jnp.sum(shading * depth_radiance, axis=0)
    opacity = 1.0 - through[-1]
    return jnp.stack([pool_pixels(total_radiance), pool_pixels(opacity)])


def solution(mesh):
    in_specs = (P("gx", None, "gy", "gz"), P("gx", "gy", "gz"), P("gx", "gy"))
    out_specs = P(None, "gx", ("gy", "gz"))
    return jax.shard_map(shards, mesh=mesh, in_specs=in_specs, out_specs=out_specs, check_vma=False)
```

profile of v0, /device:TPU:2, one launch (start us, length us, event | category | flops | bytes accessed | tf_op | source)
XLA Modules:
  0.0 112.2 jit_solution(17668879793202526838)
XLA Ops:
  0.0 0.7 copy-done.3
  0.9 0.6 scatter_custom_fusion.2
  1.6 0.6 scatter_custom_fusion.3
  2.2 5.9 %collective-permute-start.2 = (s32[2]{0:T(128)S(1)}, s32[2]{0:T(128)S(1)}, u32[]{:S(2)}, u32[]{:S(2)}) collective-permute-start(s32[2]{0:T(128)S(1)} %scatter_custom_fusion.3), channel_id=1, source_target_pairs={{0,224},{16,240},{32,0},{48,16},{64,32},{80,48},{96,64},{112,80},{... | collective-permute-start | bytes 32 | tf_op jit(solution)/shard_map/ppermute | solution.py:19
  8.7 1.5 %collective-permute-start = (s32[2]{0:T(128)S(1)}, s32[2]{0:T(128)S(1)}, u32[]{:S(2)}, u32[]{:S(2)}) collective-permute-start(s32[2]{0:T(128)S(1)} %scatter_custom_fusion.1), channel_id=1, source_target_pairs={{0,240},{16,0},{32,16},{48,32},{64,48},{80,64},{96,80},{112,96},{1... | collective-permute-start | bytes 32 | tf_op jit(solution)/shard_map/ppermute | solution.py:19
  10.2 0.6 scatter_custom_fusion.4
  10.9 1.4 %reduce_max.22 = f32[8,32]{1,0:T(8,128)S(1)} reduce(f32[8,8,32,128]{3,2,1,0:T(8,128)} %param.3, f32[]{:T(128)} %constant.125.clone.1), dimensions={1,3}, to_apply=%region_6.7 | reduce | flops 261888 | bytes 1049604 | tf_op jit(solution)/shard_map/reduce_max | solution.py:43
  13.1 1.5 %collective-permute-start.8 = (f32[2,1,4]{2,0,1:T(2,128)S(1)}, f32[2,1,4]{2,0,1:T(2,128)S(1)}, u32[]{:S(2)}, u32[]{:S(2)}) collective-permute-start(f32[2,1,4]{2,0,1:T(2,128)S(1)} %bitcast.148), channel_id=1, source_target_pairs={{0,240},{16,0},{32,16},{48,32},{64,48},{80,64},{96,80},{112,96},{1... | collective-permute-start | bytes 104 | tf_op jit(solution)/shard_map/ppermute | solution.py:19
  14.8 0.6 scatter_custom_fusion
  18.0 2.1 %collective-permute-start.10 = (f32[2,1,4]{2,0,1:T(2,128)S(1)}, f32[2,1,4]{2,0,1:T(2,128)S(1)}, u32[]{:S(2)}, u32[]{:S(2)}) collective-permute-start(f32[2,1,4]{2,0,1:T(2,128)S(1)} %bitcast.150), channel_id=1, source_target_pairs={{0,224},{16,240},{32,0},{48,16},{64,32},{80,48},{96,64},{112,80},{... | collective-permute-start | bytes 104 | tf_op jit(solution)/shard_map/ppermute | solution.py:19
  23.8 3.5 %collective-permute-start.6 = (s32[2,8,32]{2,1,0:T(8,128)S(1)}, s32[2,8,32]{2,1,0:T(8,128)S(1)}, u32[]{:S(2)}, u32[]{:S(2)}) collective-permute-start(s32[2,8,32]{2,1,0:T(8,128)S(1)} %gather_fusion.4), channel_id=1, source_target_pairs={{0,240},{16,0},{32,16},{48,32},{64,48},{80,64},{96,80},{112,96},{1... | collective-permute-start | bytes 6152 | tf_op jit(solution)/shard_map/ppermute | solution.py:19
  27.5 1.7 %collective-permute-start.4 = (s32[2,8,32]{2,1,0:T(8,128)S(1)}, s32[2,8,32]{2,1,0:T(8,128)S(1)}, u32[]{:S(2)}, u32[]{:S(2)}) collective-permute-start(s32[2,8,32]{2,1,0:T(8,128)S(1)} %gather_fusion), channel_id=1, source_target_pairs={{0,224},{16,240},{32,0},{48,16},{64,32},{80,48},{96,64},{112,80},{... | collective-permute-start | bytes 6152 | tf_op jit(solution)/shard_map/ppermute | solution.py:19
  29.6 0.6 scatter_custom_fusion.10
  30.3 10.7 %pmax.7 = f32[8,1,4]{0,2,1:T(4,128)S(1)} all-reduce(f32[8,1,4]{0,2,1:T(4,128)S(1)} %bitcast.135), channel_id=1, replica_groups=mesh['gx'=16,'gy'=4,'gz'=4] {'gz'}, use_global_device_ids=true, to_apply=%region_14.15 | all-reduce | flops 32 | bytes 256 | tf_op jit(solution)/shard_map/pmax | solution.py:47
  44.5 4.2 %collective-permute-done.15 = f32[2,1,4]{2,0,1:T(2,128)S(1)} collective-permute-done((f32[2,1,4]{2,0,1:T(2,128)S(1)}, f32[2,1,4]{2,0,1:T(2,128)S(1)}, u32[]{:S(2)}, u32[]{:S(2)}) %collective-permute-start.15) | collective-permute-done | bytes 64 | tf_op jit(solution)/shard_map/ppermute | solution.py:19
  49.2 0.7 collective-permute-done.14
  50.5 4.2 %collective-permute-done.13 = f32[2,1,4]{2,0,1:T(2,128)S(1)} collective-permute-done((f32[2,1,4]{2,0,1:T(2,128)S(1)}, f32[2,1,4]{2,0,1:T(2,128)S(1)}, u32[]{:S(2)}, u32[]{:S(2)}) %collective-permute-start.13) | collective-permute-done | bytes 64 | tf_op jit(solution)/shard_map/ppermute | solution.py:19
  55.3 3.0 %collective-permute-done.12 = f32[2,1,4]{2,0,1:T(2,128)S(1)} collective-permute-done((f32[2,1,4]{2,0,1:T(2,128)S(1)}, f32[2,1,4]{2,0,1:T(2,128)S(1)}, u32[]{:S(2)}, u32[]{:S(2)}) %collective-permute-start.12) | collective-permute-done | bytes 64 | tf_op jit(solution)/shard_map/ppermute | solution.py:19
  62.8 0.7 scatter_fusion.7
  63.6 0.6 collective-permute-start.20
  64.2 0.7 scatter_fusion.6
  65.0 0.7 scatter_fusion.8
  65.8 0.7 scatter_fusion.9
  66.5 1.2 %collective-permute-start.22 = (f32[2,8,32]{2,1,0:T(8,128)S(1)}, f32[2,8,32]{2,1,0:T(8,128)S(1)}, u32[]{:S(2)}, u32[]{:S(2)}) collective-permute-start(f32[2,8,32]{2,1,0:T(8,128)S(1)} %scatter_fusion.9), channel_id=1, source_target_pairs={{0,224},{16,240},{32,0},{48,16},{64,32},{80,48},{96,64},{112,80},{... | collective-permute-start | bytes 6152 | tf_op jit(solution)/shard_map/ppermute | solution.py:19
  67.7 0.7 scatter_fusion.10
  68.4 1.2 %collective-permute-start.23 = (f32[2,8,32]{2,1,0:T(8,128)S(1)}, f32[2,8,32]{2,1,0:T(8,128)S(1)}, u32[]{:S(2)}, u32[]{:S(2)}) collective-permute-start(f32[2,8,32]{2,1,0:T(8,128)S(1)} %scatter_fusion.10), channel_id=1, source_target_pairs={{0,32},{16,48},{32,64},{48,80},{64,96},{80,112},{96,128},{112,144}... | collective-permute-start | bytes 6152 | tf_op jit(solution)/shard_map/ppermute | solution.py:19
  69.7 0.7 scatter_fusion.1
  70.4 3.6 %collective-permute-start.16 = (f32[2,8,32]{2,1,0:T(8,128)S(1)}, f32[2,8,32]{2,1,0:T(8,128)S(1)}, u32[]{:S(2)}, u32[]{:S(2)}) collective-permute-start(f32[2,8,32]{2,1,0:T(8,128)S(1)} %scatter_fusion.1), channel_id=1, source_target_pairs={{0,240},{16,0},{32,16},{48,32},{64,48},{80,64},{96,80},{112,96},{1... | collective-permute-start | bytes 6152 | tf_op jit(solution)/shard_map/ppermute | solution.py:19
  74.0 0.7 scatter_fusion
  74.8 0.7 scatter_fusion.2
  75.6 0.7 scatter_fusion.3
  76.3 0.7 scatter_fusion.4
  77.1 4.3 %collective-permute-done.17 = f32[2,8,32]{2,1,0:T(8,128)S(1)} collective-permute-done((f32[2,8,32]{2,1,0:T(8,128)S(1)}, f32[2,8,32]{2,1,0:T(8,128)S(1)}, u32[]{:S(2)}, u32[]{:S(2)}) %collective-permute-start.17) | collective-permute-done | bytes 2080 | tf_op jit(solution)/shard_map/ppermute | solution.py:19
  81.4 3.6 %collective-permute-done.18 = f32[2,8,32]{2,1,0:T(8,128)S(1)} collective-permute-done((f32[2,8,32]{2,1,0:T(8,128)S(1)}, f32[2,8,32]{2,1,0:T(8,128)S(1)}, u32[]{:S(2)}, u32[]{:S(2)}) %collective-permute-start.18) | collective-permute-done | bytes 2080 | tf_op jit(solution)/shard_map/ppermute | solution.py:19
  85.0 4.9 %collective-permute-done.19 = f32[2,8,32]{2,1,0:T(8,128)S(1)} collective-permute-done((f32[2,8,32]{2,1,0:T(8,128)S(1)}, f32[2,8,32]{2,1,0:T(8,128)S(1)}, u32[]{:S(2)}, u32[]{:S(2)}) %collective-permute-start.19) | collective-permute-done | bytes 2080 | tf_op jit(solution)/shard_map/ppermute | solution.py:19
  89.9 0.9 scatter_fusion.5
  91.4 0.7 reduce.8
  92.1 0.7 reshape.1071
  92.7 3.2 %all-to-all-start = ((f32[4,1,512]{2,1,0:T(1,128)}), f32[4,1,512]{2,1,0:T(1,128)S(1)}, u32[]{:S(2)}, u32[]{:S(2)}) async-start(f32[4,1,512]{2,1,0:T(1,128)} %reshape.1071), calls=%async_computation | async-start | bytes 16384 | tf_op jit(solution)/shard_map/all_to_all | solution.py:160
  96.1 0.9 scatter_fusion.11
  97.0 0.7 reduce.10
  97.7 0.7 reshape.1073
  98.4 2.9 %all-to-all-done = f32[4,1,512]{2,1,0:T(1,128)S(1)} async-done(((f32[4,1,512]{2,1,0:T(1,128)}), f32[4,1,512]{2,1,0:T(1,128)S(1)}, u32[]{:S(2)}, u32[]{:S(2)}) %all-to-all-start) | async-done | bytes 8224 | tf_op jit(solution)/shard_map/all_to_all | solution.py:160
  101.3 3.2 %all-to-all-start.1 = ((f32[4,1,512]{2,1,0:T(1,128)}), f32[4,1,512]{2,1,0:T(1,128)S(1)}, u32[]{:S(2)}, u32[]{:S(2)}) async-start(f32[4,1,512]{2,1,0:T(1,128)} %reshape.1073), calls=%async_computation.1 | async-start | bytes 16384 | tf_op jit(solution)/shard_map/all_to_all | solution.py:159
  104.5 0.7 reduce.9
  106.0 3.8 %all-to-all-done.1 = f32[4,1,512]{2,1,0:T(1,128)S(1)} async-done(((f32[4,1,512]{2,1,0:T(1,128)}), f32[4,1,512]{2,1,0:T(1,128)S(1)}, u32[]{:S(2)}, u32[]{:S(2)}) %all-to-all-start.1) | async-done | bytes 8224 | tf_op jit(solution)/shard_map/all_to_all | solution.py:159
  109.8 0.7 reduce.11
  110.6 0.6 slice-done
  (148 shorter events, 20.8 us)
Async XLA Ops:
  0.0 0.7 copy-start.3
  1.5 16.4 %collective-permute-start.1 = (s32[2]{0:T(128)S(1)}, s32[2]{0:T(128)S(1)}, u32[]{:S(2)}, u32[]{:S(2)}) collective-permute-start(s32[2]{0:T(128)S(1)} %scatter_custom_fusion.2), channel_id=1, source_target_pairs={{0,16},{16,32},{32,48},{48,64},{64,80},{80,96},{96,112},{112,128},... | collective-permute-start | bytes 32 | tf_op jit(solution)/shard_map/ppermute | solution.py:19
  2.2 15.8 %collective-permute-start.2 = (s32[2]{0:T(128)S(1)}, s32[2]{0:T(128)S(1)}, u32[]{:S(2)}, u32[]{:S(2)}) collective-permute-start(s32[2]{0:T(128)S(1)} %scatter_custom_fusion.3), channel_id=1, source_target_pairs={{0,224},{16,240},{32,0},{48,16},{64,32},{80,48},{96,64},{112,80},{... | collective-permute-start | bytes 32 | tf_op jit(solution)/shard_map/ppermute | solution.py:19
  8.7 12.5 %collective-permute-start = (s32[2]{0:T(128)S(1)}, s32[2]{0:T(128)S(1)}, u32[]{:S(2)}, u32[]{:S(2)}) collective-permute-start(s32[2]{0:T(128)S(1)} %scatter_custom_fusion.1), channel_id=1, source_target_pairs={{0,240},{16,0},{32,16},{48,32},{64,48},{80,64},{96,80},{112,96},{1... | collective-permute-start | bytes 32 | tf_op jit(solution)/shard_map/ppermute | solution.py:19
  10.8 50.9 %copy-start = (f32[8,8,32,128]{3,2,1,0:T(8,128)S(1)}, f32[8,8,32,128]{3,2,1,0:T(8,128)}, u32[]{:S(2)}) copy-start(f32[8,8,32,128]{3,2,1,0:T(8,128)} %param.3) | copy-start | bytes 3145732
  10.8 11.7 %collective-permute-start.3 = (s32[2]{0:T(128)S(1)}, s32[2]{0:T(128)S(1)}, u32[]{:S(2)}, u32[]{:S(2)}) collective-permute-start(s32[2]{0:T(128)S(1)} %scatter_custom_fusion.4), channel_id=1, source_target_pairs={{0,32},{16,48},{32,64},{48,80},{64,96},{80,112},{96,128},{112,144}... | collective-permute-start | bytes 32 | tf_op jit(solution)/shard_map/ppermute | solution.py:19
  12.4 2.3 %copy-start.2 = (s32[64,32]{0,1:T(8,128)S(1)}, s32[64,32]{0,1:T(8,128)}, u32[]{:S(2)}) copy-start(s32[64,32]{0,1:T(8,128)} %param.5) | copy-start | bytes 24580
  13.1 10.7 %collective-permute-start.8 = (f32[2,1,4]{2,0,1:T(2,128)S(1)}, f32[2,1,4]{2,0,1:T(2,128)S(1)}, u32[]{:S(2)}, u32[]{:S(2)}) collective-permute-start(f32[2,1,4]{2,0,1:T(2,128)S(1)} %bitcast.148), channel_id=1, source_target_pairs={{0,240},{16,0},{32,16},{48,32},{64,48},{80,64},{96,80},{112,96},{1... | collective-permute-start | bytes 104 | tf_op jit(solution)/shard_map/ppermute | solution.py:19
  17.9 9.5 %collective-permute-start.9 = (f32[2,1,4]{2,0,1:T(2,128)S(1)}, f32[2,1,4]{2,0,1:T(2,128)S(1)}, u32[]{:S(2)}, u32[]{:S(2)}) collective-permute-start(f32[2,1,4]{2,0,1:T(2,128)S(1)} %bitcast.151), channel_id=1, source_target_pairs={{0,16},{16,32},{32,48},{48,64},{64,80},{80,96},{96,112},{112,128},... | collective-permute-start | bytes 104 | tf_op jit(solution)/shard_map/ppermute | solution.py:19
  18.0 9.5 %collective-permute-start.10 = (f32[2,1,4]{2,0,1:T(2,128)S(1)}, f32[2,1,4]{2,0,1:T(2,128)S(1)}, u32[]{:S(2)}, u32[]{:S(2)}) collective-permute-start(f32[2,1,4]{2,0,1:T(2,128)S(1)} %bitcast.150), channel_id=1, source_target_pairs={{0,224},{16,240},{32,0},{48,16},{64,32},{80,48},{96,64},{112,80},{... | collective-permute-start | bytes 104 | tf_op jit(solution)/shard_map/ppermute | solution.py:19
  21.2 8.1 %collective-permute-start.11 = (f32[2,1,4]{2,0,1:T(2,128)S(1)}, f32[2,1,4]{2,0,1:T(2,128)S(1)}, u32[]{:S(2)}, u32[]{:S(2)}) collective-permute-start(f32[2,1,4]{2,0,1:T(2,128)S(1)} %bitcast.149), channel_id=1, source_target_pairs={{0,32},{16,48},{32,64},{48,80},{64,96},{80,112},{96,128},{112,144}... | collective-permute-start | bytes 104 | tf_op jit(solution)/shard_map/ppermute | solution.py:19
  22.5 36.7 %collective-permute-start.5 = (s32[2,8,32]{2,1,0:T(8,128)S(1)}, s32[2,8,32]{2,1,0:T(8,128)S(1)}, u32[]{:S(2)}, u32[]{:S(2)}) collective-permute-start(s32[2,8,32]{2,1,0:T(8,128)S(1)} %gather_fusion.2), channel_id=1, source_target_pairs={{0,32},{16,48},{32,64},{48,80},{64,96},{80,112},{96,128},{112,144}... | collective-permute-start | bytes 6152 | tf_op jit(solution)/shard_map/ppermute | solution.py:19
  23.8 36.0 %collective-permute-start.6 = (s32[2,8,32]{2,1,0:T(8,128)S(1)}, s32[2,8,32]{2,1,0:T(8,128)S(1)}, u32[]{:S(2)}, u32[]{:S(2)}) collective-permute-start(s32[2,8,32]{2,1,0:T(8,128)S(1)} %gather_fusion.4), channel_id=1, source_target_pairs={{0,240},{16,0},{32,16},{48,32},{64,48},{80,64},{96,80},{112,96},{1... | collective-permute-start | bytes 6152 | tf_op jit(solution)/shard_map/ppermute | solution.py:19
  27.4 32.9 %collective-permute-start.7 = (s32[2,8,32]{2,1,0:T(8,128)S(1)}, s32[2,8,32]{2,1,0:T(8,128)S(1)}, u32[]{:S(2)}, u32[]{:S(2)}) collective-permute-start(s32[2,8,32]{2,1,0:T(8,128)S(1)} %gather_fusion.6), channel_id=1, source_target_pairs={{0,16},{16,32},{32,48},{48,64},{64,80},{80,96},{96,112},{112,128},... | collective-permute-start | bytes 6152 | tf_op jit(solution)/shard_map/ppermute | solution.py:19
  27.5 33.4 %collective-permute-start.4 = (s32[2,8,32]{2,1,0:T(8,128)S(1)}, s32[2,8,32]{2,1,0:T(8,128)S(1)}, u32[]{:S(2)}, u32[]{:S(2)}) collective-permute-start(s32[2,8,32]{2,1,0:T(8,128)S(1)} %gather_fusion), channel_id=1, source_target_pairs={{0,224},{16,240},{32,0},{48,16},{64,32},{80,48},{96,64},{112,80},{... | collective-permute-start | bytes 6152 | tf_op jit(solution)/shard_map/ppermute | solution.py:19
  44.4 4.2 %collective-permute-start.15 = (f32[2,1,4]{2,0,1:T(2,128)S(1)}, f32[2,1,4]{2,0,1:T(2,128)S(1)}, u32[]{:S(2)}, u32[]{:S(2)}) collective-permute-start(f32[2,1,4]{2,0,1:T(2,128)S(1)} %bitcast.141), channel_id=1, source_target_pairs={{0,16},{16,32},{32,48},{48,64},{64,80},{80,96},{96,112},{112,128},... | collective-permute-start | bytes 104 | tf_op jit(solution)/shard_map/ppermute | solution.py:19
  48.6 1.3 %collective-permute-start.14 = (f32[2,1,4]{2,0,1:T(2,128)S(1)}, f32[2,1,4]{2,0,1:T(2,128)S(1)}, u32[]{:S(2)}, u32[]{:S(2)}) collective-permute-start(f32[2,1,4]{2,0,1:T(2,128)S(1)} %bitcast.140), channel_id=1, source_target_pairs={{0,240},{16,0},{32,16},{48,32},{64,48},{80,64},{96,80},{112,96},{1... | collective-permute-start | bytes 104 | tf_op jit(solution)/shard_map/ppermute | solution.py:19
  49.9 4.8 %collective-permute-start.13 = (f32[2,1,4]{2,0,1:T(2,128)S(1)}, f32[2,1,4]{2,0,1:T(2,128)S(1)}, u32[]{:S(2)}, u32[]{:S(2)}) collective-permute-start(f32[2,1,4]{2,0,1:T(2,128)S(1)} %bitcast.139), channel_id=1, source_target_pairs={{0,32},{16,48},{32,64},{48,80},{64,96},{80,112},{96,128},{112,144}... | collective-permute-start | bytes 104 | tf_op jit(solution)/shard_map/ppermute | solution.py:19
  54.7 3.6 %collective-permute-start.12 = (f32[2,1,4]{2,0,1:T(2,128)S(1)}, f32[2,1,4]{2,0,1:T(2,128)S(1)}, u32[]{:S(2)}, u32[]{:S(2)}) collective-permute-start(f32[2,1,4]{2,0,1:T(2,128)S(1)} %bitcast.138), channel_id=1, source_target_pairs={{0,224},{16,240},{32,0},{48,16},{64,32},{80,48},{96,64},{112,80},{... | collective-permute-start | bytes 104 | tf_op jit(solution)/shard_map/ppermute | solution.py:19
  63.6 32.4 %collective-permute-start.20 = (f32[2,8,32]{2,1,0:T(8,128)S(1)}, f32[2,8,32]{2,1,0:T(8,128)S(1)}, u32[]{:S(2)}, u32[]{:S(2)}) collective-permute-start(f32[2,8,32]{2,1,0:T(8,128)S(1)} %scatter_fusion.7), channel_id=1, source_target_pairs={{0,240},{16,0},{32,16},{48,32},{64,48},{80,64},{96,80},{112,96},{1... | collective-permute-start | bytes 6152 | tf_op jit(solution)/shard_map/ppermute | solution.py:19
  65.7 30.3 %collective-permute-start.21 = (f32[2,8,32]{2,1,0:T(8,128)S(1)}, f32[2,8,32]{2,1,0:T(8,128)S(1)}, u32[]{:S(2)}, u32[]{:S(2)}) collective-permute-start(f32[2,8,32]{2,1,0:T(8,128)S(1)} %scatter_fusion.8), channel_id=1, source_target_pairs={{0,16},{16,32},{32,48},{48,64},{64,80},{80,96},{96,112},{112,128},... | collective-permute-start | bytes 6152 | tf_op jit(solution)/shard_map/ppermute | solution.py:19
  66.5 29.5 %collective-permute-start.22 = (f32[2,8,32]{2,1,0:T(8,128)S(1)}, f32[2,8,32]{2,1,0:T(8,128)S(1)}, u32[]{:S(2)}, u32[]{:S(2)}) collective-permute-start(f32[2,8,32]{2,1,0:T(8,128)S(1)} %scatter_fusion.9), channel_id=1, source_target_pairs={{0,224},{16,240},{32,0},{48,16},{64,32},{80,48},{96,64},{112,80},{... | collective-permute-start | bytes 6152 | tf_op jit(solution)/shard_map/ppermute | solution.py:19
  68.4 27.6 %collective-permute-start.23 = (f32[2,8,32]{2,1,0:T(8,128)S(1)}, f32[2,8,32]{2,1,0:T(8,128)S(1)}, u32[]{:S(2)}, u32[]{:S(2)}) collective-permute-start(f32[2,8,32]{2,1,0:T(8,128)S(1)} %scatter_fusion.10), channel_id=1, source_target_pairs={{0,32},{16,48},{32,64},{48,80},{64,96},{80,112},{96,128},{112,144}... | collective-permute-start | bytes 6152 | tf_op jit(solution)/shard_map/ppermute | solution.py:19
  70.4 6.6 %collective-permute-start.16 = (f32[2,8,32]{2,1,0:T(8,128)S(1)}, f32[2,8,32]{2,1,0:T(8,128)S(1)}, u32[]{:S(2)}, u32[]{:S(2)}) collective-permute-start(f32[2,8,32]{2,1,0:T(8,128)S(1)} %scatter_fusion.1), channel_id=1, source_target_pairs={{0,240},{16,0},{32,16},{48,32},{64,48},{80,64},{96,80},{112,96},{1... | collective-permute-start | bytes 6152 | tf_op jit(solution)/shard_map/ppermute | solution.py:19
  77.1 4.3 %collective-permute-start.17 = (f32[2,8,32]{2,1,0:T(8,128)S(1)}, f32[2,8,32]{2,1,0:T(8,128)S(1)}, u32[]{:S(2)}, u32[]{:S(2)}) collective-permute-start(f32[2,8,32]{2,1,0:T(8,128)S(1)} %scatter_fusion.2), channel_id=1, source_target_pairs={{0,16},{16,32},{32,48},{48,64},{64,80},{80,96},{96,112},{112,128},... | collective-permute-start | bytes 6152 | tf_op jit(solution)/shard_map/ppermute | solution.py:19
  81.4 3.7 %collective-permute-start.18 = (f32[2,8,32]{2,1,0:T(8,128)S(1)}, f32[2,8,32]{2,1,0:T(8,128)S(1)}, u32[]{:S(2)}, u32[]{:S(2)}) collective-permute-start(f32[2,8,32]{2,1,0:T(8,128)S(1)} %scatter_fusion.3), channel_id=1, source_target_pairs={{0,224},{16,240},{32,0},{48,16},{64,32},{80,48},{96,64},{112,80},{... | collective-permute-start | bytes 6152 | tf_op jit(solution)/shard_map/ppermute | solution.py:19
  85.0 4.9 %collective-permute-start.19 = (f32[2,8,32]{2,1,0:T(8,128)S(1)}, f32[2,8,32]{2,1,0:T(8,128)S(1)}, u32[]{:S(2)}, u32[]{:S(2)}) collective-permute-start(f32[2,8,32]{2,1,0:T(8,128)S(1)} %scatter_fusion.4), channel_id=1, source_target_pairs={{0,32},{16,48},{32,64},{48,80},{64,96},{80,112},{96,128},{112,144}... | collective-permute-start | bytes 6152 | tf_op jit(solution)/shard_map/ppermute | solution.py:19
  92.7 8.5 %all-to-all-start = ((f32[4,1,512]{2,1,0:T(1,128)}), f32[4,1,512]{2,1,0:T(1,128)S(1)}, u32[]{:S(2)}, u32[]{:S(2)}) async-start(f32[4,1,512]{2,1,0:T(1,128)} %reshape.1071), calls=%async_computation | async-start | bytes 16384 | tf_op jit(solution)/shard_map/all_to_all | solution.py:160
  101.3 8.5 %all-to-all-start.1 = ((f32[4,1,512]{2,1,0:T(1,128)}), f32[4,1,512]{2,1,0:T(1,128)S(1)}, u32[]{:S(2)}, u32[]{:S(2)}) async-start(f32[4,1,512]{2,1,0:T(1,128)} %reshape.1073), calls=%async_computation.1 | async-start | bytes 16384 | tf_op jit(solution)/shard_map/all_to_all | solution.py:159
  105.4 0.6 copy-start.1
  110.5 0.7 slice-start
where the time goes:
time: 113 us; the launch traced here: 112 us
  local copies, waits for them, and re-layouts  32.5 us (29%)
  waiting for transfers between devices  31.6 us (28%)
  starting transfers between devices  29.7 us (26%)
  blocking collectives  10.7 us (9%)
  other arithmetic  6.13 us (5%)
    ppermute x24, waiting for transfers between devices, shifted(): return lax.ppermute(value, axis, pairs)  25 us
    ppermute x24, starting transfers between devices, shifted(): return lax.ppermute(value, axis, pairs)  23.2 us
    scatter x20, local copies, waits for them, and re-layouts, place_rows(): return empty_rows.at[targets].set(values, mode='drop')  12.9 us
    pmax x1, blocking collectives, share_peaks(): return lax.pmax(peak_tiles, 'gz')  10.7 us
    gather x10, local copies, waits for them, and re-layouts, shards(): reply = (home_peaks[lookup], offsets_home[lookup])  5.53 us
    all_to_all x1, waiting for transfers between devices, shards(): lax.all_to_all(column_radiance, 'gz', split_axis=2, concat_axis=0, tiled=...  3.82 us
    unnamed x22, local copies, waits for them, and re-layouts  3.38 us
    all_to_all x1, starting transfers between devices, shards(): lax.all_to_all(column_transmit, 'gz', split_axis=2, concat_axis=0, tiled=...  3.25 us
  transfers between devices with their start and end apart: 26, of which 9 were waited for; matrix products, arithmetic and copies ran while one was open for 29% of the time, Pallas kernels for 0%

commit v1 on v0

v1 whole, which is shorter than its diff:
```python
import jax
import jax.numpy as jnp
from jax import lax
from jax.experimental import pallas as pl
from jax.experimental.pallas import tpu as pltpu
from jax.sharding import PartitionSpec as P

STRIDE = 16
MT = 8
PIXEL = 4
GLOW = 5.0
DEPTH_GAIN = 12.0

BRICKS = 8
ROWS = 32
QUARTERS = 4
CAP = 2
GROUP = 16
LAYERS = 4
NONE = BRICKS

EXCHANGES = ((2, 2, 1), (1, 1, 1), (2, 2, 0), (1, 1, 0))


def partner_of(position, exchange):
    distance, bit, up = exchange
    goes_up = ((position // bit) % 2) == up
    if isinstance(position, int):
        return (position + (distance if goes_up else -distance)) % GROUP
    step = jnp.where(goes_up, distance, GROUP - distance)
    return lax.rem(position + step, GROUP)


def find_bricks(home_ref, target):
    first = jnp.int32(NONE)
    second = jnp.int32(NONE)
    for brick in range(BRICKS - 1, -1, -1):
        hit = (home_ref[brick] >> 3) == target
        second = jnp.where(hit, first, second)
        first = jnp.where(hit, jnp.int32(brick), first)
    return first, second


def slot_label(home_ref, brick):
    held = home_ref[jnp.minimum(brick, BRICKS - 1)] & (BRICKS - 1)
    return jnp.where(brick < BRICKS, held, NONE)


def pack_kernel(home_ref, dens_ref, *refs):
    outs, sems = refs[: len(EXCHANGES)], refs[len(EXCHANGES)]
    position = lax.axis_index("gx")
    row = lax.broadcasted_iota(jnp.int32, (8, 128), 0)
    copies = []
    for number, exchange in enumerate(EXCHANGES):
        target = partner_of(position, exchange)
        bricks = find_bricks(home_ref, target)
        for place, brick in enumerate(bricks):
            copy = pltpu.make_async_copy(
                dens_ref.at[jnp.minimum(brick, BRICKS - 1)],
                outs[number].at[pl.ds(place * ROWS, ROWS)],
                sems.at[number, place],
            )
            copies.append(copy)
            copy.start()
        labels = [slot_label(home_ref, brick) for brick in bricks]
        outs[number][CAP * ROWS] = jnp.where(row == 0, labels[0], labels[1]).astype(jnp.float32)
    for copy in copies:
        copy.wait()


def select_kernel(home_ref, jitter_ref, dens_ref, *refs):
    arrived = refs[: len(EXCHANGES)]
    out_ref, own_ref, sample_ref, peak_ref, sems = refs[len(EXCHANGES) :]
    position = lax.axis_index("gx")
    own_bricks = find_bricks(home_ref, position)
    copies = []
    for place, brick in enumerate(own_bricks):
        copy = pltpu.make_async_copy(
            dens_ref.at[jnp.minimum(brick, BRICKS - 1)],
            own_ref.at[pl.ds(place * ROWS, ROWS)],
            sems.at[place],
        )
        copy.start()
        copies.append(copy)
    lane = lax.broadcasted_iota(jnp.int32, (8, 128), 1)
    plane = (lane >> 3) & 7
    collision = (lane & 7) * STRIDE
    jitter = jnp.concatenate([jitter_ref[...], jitter_ref[...]], axis=1)

    def handle(source_ref, place, slot):
        @pl.when(slot < BRICKS)
        def _():
            for quarter in range(QUARTERS):
                moved = jnp.take_along_axis(
                    jitter[quarter * 8 : (quarter + 1) * 8],
                    slot * 8 + plane,
                    axis=1,
                    mode="promise_in_bounds",
                )
                where_at = collision + moved
                samples = None
                peak = None
                for x in range(8):
                    cells = source_ref[place * ROWS + x * QUARTERS + quarter]
                    taken = jnp.take_along_axis(cells, where_at, axis=1, mode="promise_in_bounds")
                    samples = taken if x == 0 else jnp.where(plane == x, taken, samples)
                    peak = cells if x == 0 else jnp.maximum(peak, cells)
                sample_ref[slot, quarter] = samples
                peak_ref[quarter, pl.ds(slot, 1), :] = jnp.max(peak, axis=0, keepdims=True)

    for source_ref in arrived:
        for place in range(CAP):
            label = source_ref[CAP * ROWS, place : place + 1, 0:1][0, 0]
            handle(source_ref, place, label.astype(jnp.int32))
    for place in range(CAP):
        copies[place].wait()
        handle(own_ref, place, slot_label(home_ref, own_bricks[place]))
    for quarter in range(QUARTERS):
        for tile in range(BRICKS // 2):
            out_ref[quarter, tile] = jnp.where(
                lane < 64, sample_ref[2 * tile, quarter], sample_ref[2 * tile + 1, quarter]
            )
        peak = jnp.max(peak_ref[quarter], axis=1, keepdims=True)
        out_ref[quarter, BRICKS // 2] = jnp.broadcast_to(peak, (8, 128))


def render_kernel(own_ref, *refs):
    others = refs[: LAYERS - 1]
    out_ref, held_ref = refs[LAYERS - 1 :]
    layer = lax.axis_index("gz")
    held_ref[layer] = own_ref[layer]
    for number, other in enumerate(others):
        held_ref[layer ^ (number + 1)] = other[...]
    lane = lax.broadcasted_iota(jnp.int32, (8, 128), 1)
    tiles = BRICKS // 2
    peak = held_ref[0, tiles]
    for depth in range(1, LAYERS):
        peak = jnp.maximum(peak, held_ref[depth, tiles])
    absorb = jnp.float32(DEPTH_GAIN / (8 * LAYERS))
    light = jnp.zeros((8, 128), jnp.float32)
    cover = jnp.zeros((8, 128), jnp.float32)
    picked = (lane & 3) * 32
    for tile in range(tiles):
        majorant = jnp.where(lane < 64, peak[2 * tile : 2 * tile + 1], peak[2 * tile + 1 : 2 * tile + 2])
        through = None
        radiance = None
        for depth in range(LAYERS):
            samples = held_ref[depth, tile]
            ratio = absorb * samples / majorant
            passed = 1.0 - ratio
            shone = ratio * (GLOW * samples)
            for span in (1, 2, 4):
                shone = shone + passed * pltpu.roll(shone, 128 - span, 1)
                passed = passed * pltpu.roll(passed, 128 - span, 1)
            if depth == 0:
                through, radiance = passed, shone
            else:
                radiance = radiance + through * shone
                through = through * passed
        opacity = 1.0 - through
        pooled = []
        for field in (radiance, opacity):
            field = field + pltpu.roll(field, 120, 1)
            field = field + pltpu.roll(field, 112, 1)
            field = field + pltpu.roll(field, 7, 0)
            field = field + pltpu.roll(field, 6, 0)
            pooled.append(jnp.take_along_axis(field, picked, axis=1, mode="promise_in_bounds"))
        here = (lane >> 2) == tile
        light = jnp.where(here, pooled[0], light)
        cover = jnp.where(here, pooled[1], cover)
    scale = jnp.float32(1.0 / (PIXEL * PIXEL))
    for number, field in enumerate((light, cover)):
        for pixel in range(8 // PIXEL):
            out_ref[number, pixel : pixel + 1, :] = field[pixel * PIXEL : pixel * PIXEL + 1, :16] * scale


def shards(sim_density, brick_home, jitter):
    home = brick_home.reshape(BRICKS)
    density = sim_density.reshape(BRICKS, ROWS, 8, 128)
    smem = pl.BlockSpec(memory_space=pltpu.SMEM)
    vmem = pl.BlockSpec(memory_space=pltpu.VMEM)
    anywhere = pl.BlockSpec(memory_space=pl.ANY)
    box = jax.ShapeDtypeStruct((CAP * ROWS + 1, 8, 128), jnp.float32)
    count = len(EXCHANGES)
    packed = pl.pallas_call(
        pack_kernel,
        out_shape=[box] * count,
        in_specs=[smem, anywhere],
        out_specs=[vmem] * count,
        scratch_shapes=[pltpu.SemaphoreType.DMA((count, CAP))],
        name="pack",
    )(home, density)
    arrived = []
    for exchange, bricks in zip(EXCHANGES, packed):
        pairs = [(source, partner_of(source, exchange)) for source in range(GROUP)]
        arrived.append(lax.ppermute(bricks, "gx", pairs))
    message = pl.pallas_call(
        select_kernel,
        out_shape=jax.ShapeDtypeStruct((QUARTERS, BRICKS // 2 + 1, 8, 128), jnp.float32),
        in_specs=[smem, vmem, anywhere] + [vmem] * count,
        out_specs=vmem,
        scratch_shapes=[
            pltpu.VMEM((CAP * ROWS, 8, 128), jnp.float32),
            pltpu.VMEM((BRICKS, QUARTERS, 8, 128), jnp.float32),
            pltpu.VMEM((QUARTERS, BRICKS, 128), jnp.float32),
            pltpu.SemaphoreType.DMA((CAP,)),
        ],
        name="select",
    )(home, jitter.T, density, *arrived)
    layer = lax.axis_index("gz")
    others = []
    for mask in range(1, LAYERS):
        sent = lax.dynamic_index_in_dim(message, layer ^ mask, 0, keepdims=False)
        others.append(lax.ppermute(sent, "gz", [(source, source ^ mask) for source in range(LAYERS)]))
    image = pl.pallas_call(
        render_kernel,
        out_shape=jax.ShapeDtypeStruct((2, 8 // PIXEL, 16), jnp.float32),
        in_specs=[vmem] * LAYERS,
        out_specs=vmem,
        scratch_shapes=[pltpu.VMEM((LAYERS, BRICKS // 2 + 1, 8, 128), jnp.float32)],
        name="render",
    )(message, *others)
    return jnp.transpose(image, (0, 2, 1))


def solution(mesh):
    in_specs = (P("gx", None, "gy", "gz"), P("gx", "gy", "gz"), P("gx", "gy"))
    out_specs = P(None, "gx", ("gy", "gz"))
    return jax.shard_map(shards, mesh=mesh, in_specs=in_specs, out_specs=out_specs, check_vma=False)
```

time: 113 us -> 37.8 us (0.33)
  local copies, waits for them, and re-layouts: 32.5 us -> 2.2 us
  starting transfers between devices: 29.7 us -> 11.8 us
  waiting for transfers between devices: 31.6 us -> 14.5 us
  blocking collectives: 10.7 us -> 0 us
  Pallas kernels: 0 us -> 8.98 us
  other arithmetic: 6.13 us -> 0 us
    scatter x25 -> x0, local copies, waits for them, and re-layouts: 15.8 us -> none  [the longest x20 12.9 us: place_rows(): return empty_rows.at[targets].set(values, mode='drop')]
    ppermute x24 -> x7, starting transfers between devices: 23.2 us -> 11.8 us  [the longest x4 7.13 us: shards(): arrived.append(lax.ppermute(bricks, 'gx', pairs))]
    gather x20 -> x0, local copies, waits for them, and re-layouts: 11.1 us -> none  [the longest x10 5.53 us: shards(): reply = (home_peaks[lookup], offsets_home[lookup])]
    pmax x1 -> x0, blocking collectives: 10.7 us -> none  [share_peaks(): return lax.pmax(peak_tiles, 'gz')]
    ppermute x24 -> x7, waiting for transfers between devices: 25 us -> 14.5 us  [the longest x4 9.76 us: shards(): arrived.append(lax.ppermute(bricks, 'gx', pairs))]
    pallas_call x0 -> x3, Pallas kernels: none -> 8.98 us  [the longest x1 3.93 us: shards(): pl.pallas_call(select_kernel, out_shape=jax.ShapeDtypeStruct((QUARTERS, B...]
    all_to_all x2 -> x0, waiting for transfers between devices: 6.67 us -> none  [the longest x1 3.82 us: shards(): lax.all_to_all(column_radiance, 'gz', split_axis=2, concat_axis=0, tiled=...]
    all_to_all x2 -> x0, starting transfers between devices: 6.48 us -> none  [the longest x1 3.25 us: shards(): lax.all_to_all(column_transmit, 'gz', split_axis=2, concat_axis=0, tiled=...]
  transfers between devices with their start and end apart: 26 -> 7, of which waited for: 9 -> 5; matrix products, arithmetic and copies ran while one was open for 29% -> 0% of each run, Pallas kernels for 0% -> 0%
where the time goes in v1:
time: 37.8 us; the launch traced here: 37.6 us
  waiting for transfers between devices  14.5 us (38%)
  starting transfers between devices  11.8 us (31%)
  Pallas kernels  8.98 us (24%)
  local copies, waits for them, and re-layouts  2.2 us (6%)
    ppermute x4, waiting for transfers between devices, shards(): arrived.append(lax.ppermute(bricks, 'gx', pairs))  9.76 us
    ppermute x4, starting transfers between devices, shards(): arrived.append(lax.ppermute(bricks, 'gx', pairs))  7.13 us
    ppermute x3, waiting for transfers between devices, shards(): lax.ppermute(sent, 'gz', [(source, source ^ mask) for source in range(LAY...  4.76 us
    ppermute x3, starting transfers between devices, shards(): lax.ppermute(sent, 'gz', [(source, source ^ mask) for source in range(LAY...  4.7 us
    pallas_call x1, Pallas kernels, shards(): pl.pallas_call(select_kernel, out_shape=jax.ShapeDtypeStruct((QUARTERS, B...  3.93 us
    pallas_call x1, Pallas kernels, shards(): pl.pallas_call(pack_kernel, out_shape=[box] * count, in_specs=[smem, anyw...  3.06 us
    pallas_call x1, Pallas kernels, shards(): pl.pallas_call(render_kernel, out_shape=jax.ShapeDtypeStruct((2, 8 // PIX...  2 us
    unnamed x14, local copies, waits for them, and re-layouts  1.42 us
  transfers between devices with their start and end apart: 7, of which 5 were waited for; matrix products, arithmetic and copies ran while one was open for 0% of the time, Pallas kernels for 0%

profile of v1, /device:TPU:2, one launch (start us, length us, event | category | flops | bytes accessed | tf_op | source)
XLA Modules:
  0.0 37.6 jit_solution(9332770970570953375)
XLA Ops:
  0.0 3.1 %pack.1 = (f32[65,8,128]{2,1,0:T(8,128)}, f32[65,8,128]{2,1,0:T(8,128)}, f32[65,8,128]{2,1,0:T(8,128)}, f32[65,8,128]{2,1,0:T(8,128)}) custom-call(s32[8]{0:T(128)} %bitcast.13, f32[8,32,8,128]{3,2,1,0:T(8,128)} %bitcast.10), custom_call_target="tpu_custom_call" | custom-call | tf_op jit(solution)/shard_map/pack/pallas_call | solution.py:185
  3.1 5.9 %collective-permute-start = (f32[65,8,128]{2,1,0:T(8,128)}, f32[65,8,128]{2,1,0:T(8,128)S(1)}, u32[]{:S(2)}, u32[]{:S(2)}) collective-permute-start(f32[65,8,128]{2,1,0:T(8,128)} %get-tuple-element.9), channel_id=1, source_target_pairs={{0,224},{16,240},{32,64},{48,80},{64,32},{80,48},{96,128},{112,144... | collective-permute-start | bytes 798728 | tf_op jit(solution)/shard_map/ppermute | solution.py:196
  9.0 0.0 collective-permute-start.1
  9.0 1.2 %collective-permute-start.2 = (f32[65,8,128]{2,1,0:T(8,128)}, f32[65,8,128]{2,1,0:T(8,128)S(1)}, u32[]{:S(2)}, u32[]{:S(2)}) collective-permute-start(f32[65,8,128]{2,1,0:T(8,128)} %get-tuple-element.11), channel_id=1, source_target_pairs={{0,32},{16,48},{32,0},{48,16},{64,96},{80,112},{96,64},{112,80},{1... | collective-permute-start | bytes 798728 | tf_op jit(solution)/shard_map/ppermute | solution.py:196
  10.2 0.0 collective-permute-start.3
  10.2 6.2 %collective-permute-done.refs_0_ = f32[65,8,128]{2,1,0:T(8,128)S(1)} collective-permute-done((f32[65,8,128]{2,1,0:T(8,128)}, f32[65,8,128]{2,1,0:T(8,128)S(1)}, u32[]{:S(2)}, u32[]{:S(2)}) %collective-permute-start) | collective-permute-done | bytes 266272 | tf_op jit(solution)/shard_map/ppermute | solution.py:196
  16.4 0.0 copy-start
  16.4 2.0 %collective-permute-done.1.refs_1_ = f32[65,8,128]{2,1,0:T(8,128)S(1)} collective-permute-done((f32[65,8,128]{2,1,0:T(8,128)}, f32[65,8,128]{2,1,0:T(8,128)S(1)}, u32[]{:S(2)}, u32[]{:S(2)}) %collective-permute-start.1) | collective-permute-done | bytes 266272 | tf_op jit(solution)/shard_map/ppermute | solution.py:196
  18.5 0.0 copy-start.1
  18.5 1.5 %collective-permute-done.2.refs_2_ = f32[65,8,128]{2,1,0:T(8,128)S(1)} collective-permute-done((f32[65,8,128]{2,1,0:T(8,128)}, f32[65,8,128]{2,1,0:T(8,128)S(1)}, u32[]{:S(2)}, u32[]{:S(2)}) %collective-permute-start.2) | collective-permute-done | bytes 266272 | tf_op jit(solution)/shard_map/ppermute | solution.py:196
  20.0 0.0 copy-start.2
  20.0 0.0 collective-permute-done.3.refs_3_
  20.0 0.0 copy-start.3
  20.0 0.0 copy-done
  20.0 0.0 copy-done.1
  20.0 0.7 %copy-done.2 = f32[65,8,128]{2,1,0:T(8,128)} copy-done((f32[65,8,128]{2,1,0:T(8,128)}, f32[65,8,128]{2,1,0:T(8,128)S(1)}, u32[]{:S(2)}) %copy-start.2) | copy-done | bytes 266264
  20.7 0.1 copy-done.3
  20.8 3.9 %select.1.own_ref = f32[4,5,8,128]{3,2,1,0:T(8,128)} custom-call(s32[8]{0:T(128)} %bitcast.14, s32[32,64]{1,0:T(8,128)} %bitcast.12, f32[8,32,8,128]{3,2,1,0:T(8,128)} %bitcast.11, f32[65,8,128]{2,1,0:T(8,128)} %copy-done, f32[65,8,128]{2,1,0:T(8,128)} %copy-done.1, f32[65,8,128]{2,1,0:T(8,128)} %copy-done.2, f32[65,8,128]{2,1,0:T(8,128)} %copy-done.3), custom_call_target="tpu_custom_call" | custom-call | tf_op jit(solution)/shard_map/select/pallas_call | solution.py:197
  24.7 0.8 %dynamic-slice_bitcast_fusion = (f32[5,8,128]{2,1,0:T(8,128)S(1)}, f32[5,8,128]{2,1,0:T(8,128)S(1)}, f32[5,8,128]{2,1,0:T(8,128)S(1)}) fusion(f32[4,5,8,128]{3,2,1,0:T(8,128)} %select.1.own_ref, s32[]{:T(128)S(6)} %select_n.12, s32[]{:T(128)S(6)} %select_n.11, s32[]{:T(128)S(6)} %select_n.10), kind=kLoop, calls=%fused_computation | loop fusion | bytes 122892 | tf_op jit(solution)/shard_map/jit(dynamic_index_in_dim)/squeeze | solution.py:213
  25.5 1.6 %collective-permute-start.4 = (f32[5,8,128]{2,1,0:T(8,128)S(1)}, f32[5,8,128]{2,1,0:T(8,128)S(1)}, u32[]{:S(2)}, u32[]{:S(2)}) collective-permute-start(f32[5,8,128]{2,1,0:T(8,128)S(1)} %get-tuple-element.15), channel_id=1, source_target_pairs={{0,1},{1,0},{2,3},{3,2},{4,5},{5,4},{6,7},{7,6},{8,9},{9,8},{10,11... | collective-permute-start | bytes 61448 | tf_op jit(solution)/shard_map/ppermute | solution.py:214
  27.1 2.9 %collective-permute-start.5 = (f32[5,8,128]{2,1,0:T(8,128)S(1)}, f32[5,8,128]{2,1,0:T(8,128)S(1)}, u32[]{:S(2)}, u32[]{:S(2)}) collective-permute-start(f32[5,8,128]{2,1,0:T(8,128)S(1)} %get-tuple-element.14), channel_id=1, source_target_pairs={{0,2},{1,3},{2,0},{3,1},{4,6},{5,7},{6,4},{7,5},{8,10},{9,11},{10,... | collective-permute-start | bytes 61448 | tf_op jit(solution)/shard_map/ppermute | solution.py:214
  30.0 0.2 collective-permute-start.6
  30.2 0.0 collective-permute-done.4.refs_0_
  30.2 0.0 copy-start.4
  30.2 2.2 %collective-permute-done.5.refs_1_ = f32[5,8,128]{2,1,0:T(8,128)S(1)} collective-permute-done((f32[5,8,128]{2,1,0:T(8,128)S(1)}, f32[5,8,128]{2,1,0:T(8,128)S(1)}, u32[]{:S(2)}, u32[]{:S(2)}) %collective-permute-start.5) | collective-permute-done | bytes 20512 | tf_op jit(solution)/shard_map/ppermute | solution.py:214
  32.3 0.0 copy-start.5
  32.3 2.6 %collective-permute-done.6.refs_2_ = f32[5,8,128]{2,1,0:T(8,128)S(1)} collective-permute-done((f32[5,8,128]{2,1,0:T(8,128)S(1)}, f32[5,8,128]{2,1,0:T(8,128)S(1)}, u32[]{:S(2)}, u32[]{:S(2)}) %collective-permute-start.6) | collective-permute-done | bytes 20512 | tf_op jit(solution)/shard_map/ppermute | solution.py:214
  35.0 0.0 copy-done.4
  35.0 0.0 copy-done.5
  35.0 0.0 copy-start.6
  35.0 0.6 %copy-done.6 = f32[5,8,128]{2,1,0:T(8,128)} copy-done((f32[5,8,128]{2,1,0:T(8,128)}, f32[5,8,128]{2,1,0:T(8,128)S(1)}, u32[]{:S(2)}) %copy-start.6) | copy-done | bytes 20504
  35.6 2.0 %render.1 = f32[2,2,16]{2,1,0:T(2,128)} custom-call(f32[4,5,8,128]{3,2,1,0:T(8,128)} %select.1.own_ref, f32[5,8,128]{2,1,0:T(8,128)} %copy-done.4, f32[5,8,128]{2,1,0:T(8,128)} %copy-done.5, f32[5,8,128]{2,1,0:T(8,128)} %copy-done.6), custom_call_target="tpu_custom_call" | custom-call | tf_op jit(solution)/shard_map/render/pallas_call | solution.py:215
Async XLA Ops:
  3.1 13.4 %collective-permute-start = (f32[65,8,128]{2,1,0:T(8,128)}, f32[65,8,128]{2,1,0:T(8,128)S(1)}, u32[]{:S(2)}, u32[]{:S(2)}) collective-permute-start(f32[65,8,128]{2,1,0:T(8,128)} %get-tuple-element.9), channel_id=1, source_target_pairs={{0,224},{16,240},{32,64},{48,80},{64,32},{80,48},{96,128},{112,144... | collective-permute-start | bytes 798728 | tf_op jit(solution)/shard_map/ppermute | solution.py:196
  9.0 9.5 %collective-permute-start.1 = (f32[65,8,128]{2,1,0:T(8,128)}, f32[65,8,128]{2,1,0:T(8,128)S(1)}, u32[]{:S(2)}, u32[]{:S(2)}) collective-permute-start(f32[65,8,128]{2,1,0:T(8,128)} %get-tuple-element.10), channel_id=1, source_target_pairs={{0,240},{16,32},{32,16},{48,64},{64,48},{80,96},{96,80},{112,128},... | collective-permute-start | bytes 798728 | tf_op jit(solution)/shard_map/ppermute | solution.py:196
  9.0 10.9 %collective-permute-start.2 = (f32[65,8,128]{2,1,0:T(8,128)}, f32[65,8,128]{2,1,0:T(8,128)S(1)}, u32[]{:S(2)}, u32[]{:S(2)}) collective-permute-start(f32[65,8,128]{2,1,0:T(8,128)} %get-tuple-element.11), channel_id=1, source_target_pairs={{0,32},{16,48},{32,0},{48,16},{64,96},{80,112},{96,64},{112,80},{1... | collective-permute-start | bytes 798728 | tf_op jit(solution)/shard_map/ppermute | solution.py:196
  10.2 9.8 %collective-permute-start.3 = (f32[65,8,128]{2,1,0:T(8,128)}, f32[65,8,128]{2,1,0:T(8,128)S(1)}, u32[]{:S(2)}, u32[]{:S(2)}) collective-permute-start(f32[65,8,128]{2,1,0:T(8,128)} %get-tuple-element.12), channel_id=1, source_target_pairs={{0,16},{16,0},{32,48},{48,32},{64,80},{80,64},{96,112},{112,96},{1... | collective-permute-start | bytes 798728 | tf_op jit(solution)/shard_map/ppermute | solution.py:196
  16.4 3.5 %copy-start = (f32[65,8,128]{2,1,0:T(8,128)}, f32[65,8,128]{2,1,0:T(8,128)S(1)}, u32[]{:S(2)}) copy-start(f32[65,8,128]{2,1,0:T(8,128)S(1)} %collective-permute-done.refs_0_) | copy-start | bytes 798724
  18.5 1.5 %copy-start.1 = (f32[65,8,128]{2,1,0:T(8,128)}, f32[65,8,128]{2,1,0:T(8,128)S(1)}, u32[]{:S(2)}) copy-start(f32[65,8,128]{2,1,0:T(8,128)S(1)} %collective-permute-done.1.refs_1_) | copy-start | bytes 798724
  20.0 0.7 %copy-start.2 = (f32[65,8,128]{2,1,0:T(8,128)}, f32[65,8,128]{2,1,0:T(8,128)S(1)}, u32[]{:S(2)}) copy-start(f32[65,8,128]{2,1,0:T(8,128)S(1)} %collective-permute-done.2.refs_2_) | copy-start | bytes 798724
  20.0 0.8 %copy-start.3 = (f32[65,8,128]{2,1,0:T(8,128)}, f32[65,8,128]{2,1,0:T(8,128)S(1)}, u32[]{:S(2)}) copy-start(f32[65,8,128]{2,1,0:T(8,128)S(1)} %collective-permute-done.3.refs_3_) | copy-start | bytes 798724
  25.5 4.7 %collective-permute-start.4 = (f32[5,8,128]{2,1,0:T(8,128)S(1)}, f32[5,8,128]{2,1,0:T(8,128)S(1)}, u32[]{:S(2)}, u32[]{:S(2)}) collective-permute-start(f32[5,8,128]{2,1,0:T(8,128)S(1)} %get-tuple-element.15), channel_id=1, source_target_pairs={{0,1},{1,0},{2,3},{3,2},{4,5},{5,4},{6,7},{7,6},{8,9},{9,8},{10,11... | collective-permute-start | bytes 61448 | tf_op jit(solution)/shard_map/ppermute | solution.py:214
  27.1 5.3 %collective-permute-start.5 = (f32[5,8,128]{2,1,0:T(8,128)S(1)}, f32[5,8,128]{2,1,0:T(8,128)S(1)}, u32[]{:S(2)}, u32[]{:S(2)}) collective-permute-start(f32[5,8,128]{2,1,0:T(8,128)S(1)} %get-tuple-element.14), channel_id=1, source_target_pairs={{0,2},{1,3},{2,0},{3,1},{4,6},{5,7},{6,4},{7,5},{8,10},{9,11},{10,... | collective-permute-start | bytes 61448 | tf_op jit(solution)/shard_map/ppermute | solution.py:214
  30.0 5.0 %collective-permute-start.6 = (f32[5,8,128]{2,1,0:T(8,128)S(1)}, f32[5,8,128]{2,1,0:T(8,128)S(1)}, u32[]{:S(2)}, u32[]{:S(2)}) collective-permute-start(f32[5,8,128]{2,1,0:T(8,128)S(1)} %get-tuple-element.13), channel_id=1, source_target_pairs={{0,3},{1,2},{2,1},{3,0},{4,7},{5,6},{6,5},{7,4},{8,11},{9,10},{10,... | collective-permute-start | bytes 61448 | tf_op jit(solution)/shard_map/ppermute | solution.py:214
  30.2 4.8 %copy-start.4 = (f32[5,8,128]{2,1,0:T(8,128)}, f32[5,8,128]{2,1,0:T(8,128)S(1)}, u32[]{:S(2)}) copy-start(f32[5,8,128]{2,1,0:T(8,128)S(1)} %collective-permute-done.4.refs_0_) | copy-start | bytes 61444
  32.3 2.6 %copy-start.5 = (f32[5,8,128]{2,1,0:T(8,128)}, f32[5,8,128]{2,1,0:T(8,128)S(1)}, u32[]{:S(2)}) copy-start(f32[5,8,128]{2,1,0:T(8,128)S(1)} %collective-permute-done.5.refs_1_) | copy-start | bytes 61444
  35.0 0.6 %copy-start.6 = (f32[5,8,128]{2,1,0:T(8,128)}, f32[5,8,128]{2,1,0:T(8,128)S(1)}, u32[]{:S(2)}) copy-start(f32[5,8,128]{2,1,0:T(8,128)S(1)} %collective-permute-done.6.refs_2_) | copy-start | bytes 61444

commit v2 on v1

v2 whole, which is shorter than its diff:
```python
import jax
import jax.numpy as jnp
from jax import lax
from jax.experimental import pallas as pl
from jax.experimental.pallas import tpu as pltpu
from jax.sharding import PartitionSpec as P

STRIDE = 16
MT = 8
PIXEL = 4
GLOW = 5.0
DEPTH_GAIN = 12.0

BRICKS = 8
ROWS = 32
QUARTERS = 4
CAP = 2
GROUP = 16
LAYERS = 4
NONE = BRICKS
VMEM_BYTES = 4 << 20

MOVES = (2, 1, -2, -1)
PLACES = len(MOVES) + 1


def find_bricks(home_ref, target):
    first = jnp.int32(NONE)
    second = jnp.int32(NONE)
    for brick in range(BRICKS - 1, -1, -1):
        hit = (home_ref[brick] >> 3) == target
        second = jnp.where(hit, first, second)
        first = jnp.where(hit, jnp.int32(brick), first)
    return first, second


def slot_label(home_ref, brick):
    held = home_ref[jnp.minimum(brick, BRICKS - 1)] & (BRICKS - 1)
    return jnp.where(brick < BRICKS, held, NONE)


def pack_kernel(home_hbm, dens_hbm, *refs):
    outs = refs[:PLACES]
    home_ref, dens_ref, home_sem, dens_sem = refs[PLACES:]
    home_copy = pltpu.make_async_copy(home_hbm, home_ref, home_sem)
    home_copy.start()
    dens_copy = pltpu.make_async_copy(dens_hbm, dens_ref, dens_sem)
    dens_copy.start()
    position = lax.axis_index("gx")
    row = lax.broadcasted_iota(jnp.int32, (8, 128), 0)
    home_copy.wait()
    chosen = []
    for move, out_ref in zip(MOVES + (0,), outs):
        bricks = find_bricks(home_ref, lax.rem(position + (move + GROUP), GROUP))
        labels = [slot_label(home_ref, brick) for brick in bricks]
        out_ref[CAP * ROWS] = jnp.where(row == 0, labels[0], labels[1]).astype(jnp.float32)
        chosen.append([jnp.minimum(brick, BRICKS - 1) for brick in bricks])
    dens_copy.wait()
    for out_ref, bricks in zip(outs, chosen):
        for place, brick in enumerate(bricks):
            out_ref[pl.ds(place * ROWS, ROWS)] = dens_ref[brick]


def select_kernel(jitter_ref, *refs):
    arrived = refs[:PLACES]
    outs = refs[PLACES : PLACES + LAYERS]
    sample_ref, peak_ref = refs[PLACES + LAYERS :]
    layer = lax.axis_index("gz")
    lane = lax.broadcasted_iota(jnp.int32, (8, 128), 1)
    plane = (lane >> 3) & 7
    collision = (lane & 7) * STRIDE
    jitter = jnp.concatenate([jitter_ref[...], jitter_ref[...]], axis=1)

    def handle(source_ref, place):
        label = source_ref[CAP * ROWS, place : place + 1, 0:1][0, 0]
        slot = label.astype(jnp.int32)

        @pl.when(slot < BRICKS)
        def _():
            for quarter in range(QUARTERS):
                moved = jnp.take_along_axis(
                    jitter[quarter * 8 : (quarter + 1) * 8],
                    slot * 8 + plane,
                    axis=1,
                    mode="promise_in_bounds",
                )
                where_at = collision + moved
                samples = None
                peak = None
                for x in range(8):
                    cells = source_ref[place * ROWS + x * QUARTERS + quarter]
                    taken = jnp.take_along_axis(cells, where_at, axis=1, mode="promise_in_bounds")
                    samples = taken if x == 0 else jnp.where(plane == x, taken, samples)
                    peak = cells if x == 0 else jnp.maximum(peak, cells)
                sample_ref[slot, quarter] = samples
                peak_ref[quarter, pl.ds(slot, 1), :] = jnp.max(peak, axis=0, keepdims=True)

    for source_ref in arrived:
        for place in range(CAP):
            handle(source_ref, place)
    for mask, out_ref in enumerate(outs):
        quarter = layer ^ mask
        for tile in range(BRICKS // 2):
            out_ref[tile] = jnp.where(
                lane < 64, sample_ref[2 * tile, quarter], sample_ref[2 * tile + 1, quarter]
            )
        peak = jnp.max(peak_ref[quarter], axis=1, keepdims=True)
        out_ref[BRICKS // 2] = jnp.broadcast_to(peak, (8, 128))


def render_kernel(*refs):
    out_ref, held_ref = refs[LAYERS:]
    layer = lax.axis_index("gz")
    for mask, message in enumerate(refs[:LAYERS]):
        held_ref[layer ^ mask] = message[...]
    lane = lax.broadcasted_iota(jnp.int32, (8, 128), 1)
    tiles = BRICKS // 2
    peak = held_ref[0, tiles]
    for depth in range(1, LAYERS):
        peak = jnp.maximum(peak, held_ref[depth, tiles])
    absorb = jnp.float32(DEPTH_GAIN / (8 * LAYERS))
    light = jnp.zeros((8, 128), jnp.float32)
    cover = jnp.zeros((8, 128), jnp.float32)
    picked = (lane & 3) * 32
    for tile in range(tiles):
        majorant = jnp.where(lane < 64, peak[2 * tile : 2 * tile + 1], peak[2 * tile + 1 : 2 * tile + 2])
        through = None
        radiance = None
        for depth in range(LAYERS):
            samples = held_ref[depth, tile]
            ratio = absorb * samples / majorant
            passed = 1.0 - ratio
            shone = ratio * (GLOW * samples)
            for span in (1, 2, 4):
                shone = shone + passed * pltpu.roll(shone, 128 - span, 1)
                passed = passed * pltpu.roll(passed, 128 - span, 1)
            if depth == 0:
                through, radiance = passed, shone
            else:
                radiance = radiance + through * shone
                through = through * passed
        opacity = 1.0 - through
        pooled = []
        for field in (radiance, opacity):
            field = field + pltpu.roll(field, 120, 1)
            field = field + pltpu.roll(field, 112, 1)
            field = field + pltpu.roll(field, 7, 0)
            field = field + pltpu.roll(field, 6, 0)
            pooled.append(jnp.take_along_axis(field, picked, axis=1, mode="promise_in_bounds"))
        here = (lane >> 2) == tile
        light = jnp.where(here, pooled[0], light)
        cover = jnp.where(here, pooled[1], cover)
    scale = jnp.float32(1.0 / (PIXEL * PIXEL))
    for number, field in enumerate((light, cover)):
        for pixel in range(8 // PIXEL):
            out_ref[number, pixel : pixel + 1, :] = field[pixel * PIXEL : pixel * PIXEL + 1, :16] * scale


def shards(sim_density, brick_home, jitter):
    home = brick_home.reshape(BRICKS)
    density = sim_density.reshape(BRICKS, ROWS, 8, 128)
    vmem = pl.BlockSpec(memory_space=pltpu.VMEM)
    hbm = pl.BlockSpec(memory_space=pltpu.HBM)
    box = jax.ShapeDtypeStruct((CAP * ROWS + 1, 8, 128), jnp.float32)
    packed = pl.pallas_call(
        pack_kernel,
        out_shape=[box] * PLACES,
        in_specs=[hbm, hbm],
        out_specs=[vmem] * PLACES,
        scratch_shapes=[
            pltpu.SMEM((BRICKS,), jnp.int32),
            pltpu.VMEM((BRICKS, ROWS, 8, 128), jnp.float32),
            pltpu.SemaphoreType.DMA,
            pltpu.SemaphoreType.DMA,
        ],
        compiler_params=pltpu.CompilerParams(vmem_limit_bytes=VMEM_BYTES),
        name="pack",
    )(home, density)
    arrived = []
    for move, bricks in zip(MOVES, packed):
        pairs = [(source, (source + move) % GROUP) for source in range(GROUP)]
        arrived.append(lax.ppermute(bricks, "gx", pairs))
    messages = pl.pallas_call(
        select_kernel,
        out_shape=[jax.ShapeDtypeStruct((BRICKS // 2 + 1, 8, 128), jnp.float32)] * LAYERS,
        in_specs=[vmem] * (1 + PLACES),
        out_specs=[vmem] * LAYERS,
        scratch_shapes=[
            pltpu.VMEM((BRICKS, QUARTERS, 8, 128), jnp.float32),
            pltpu.VMEM((QUARTERS, BRICKS, 128), jnp.float32),
        ],
        compiler_params=pltpu.CompilerParams(vmem_limit_bytes=VMEM_BYTES),
        name="select",
    )(jitter.T, packed[-1], *arrived)
    others = []
    for mask in range(1, LAYERS):
        pairs = [(source, source ^ mask) for source in range(LAYERS)]
        others.append(lax.ppermute(messages[mask], "gz", pairs))
    image = pl.pallas_call(
        render_kernel,
        out_shape=jax.ShapeDtypeStruct((2, 8 // PIXEL, 16), jnp.float32),
        in_specs=[vmem] * LAYERS,
        out_specs=vmem,
        scratch_shapes=[pltpu.VMEM((LAYERS, BRICKS // 2 + 1, 8, 128), jnp.float32)],
        compiler_params=pltpu.CompilerParams(vmem_limit_bytes=VMEM_BYTES),
        name="render",
    )(messages[0], *others)
    return jnp.transpose(image, (0, 2, 1))


def solution(mesh):
    in_specs = (P("gx", None, "gy", "gz"), P("gx", "gy", "gz"), P("gx", "gy"))
    out_specs = P(None, "gx", ("gy", "gz"))
    return jax.shard_map(shards, mesh=mesh, in_specs=in_specs, out_specs=out_specs, check_vma=False)
```

time: 37.8 us -> 30.7 us (0.81)
  Pallas kernels: 8.98 us -> 3.96 us
  waiting for transfers between devices: 14.5 us -> 12.5 us
  starting transfers between devices: 11.8 us -> 12.2 us
    pallas_call x2, Pallas kernels: 6.98 us -> 2.87 us  [the longest x1 2.15 us: shards(): pl.pallas_call(select_kernel, out_shape=[jax.ShapeDtypeStruct((BRICKS //...]
    ppermute x4, waiting for transfers between devices: 9.76 us -> 7.74 us  [shards(): arrived.append(lax.ppermute(bricks, 'gx', pairs))]
    pallas_call x1, Pallas kernels: 2 us -> 1.09 us  [shards(): pl.pallas_call(render_kernel, out_shape=jax.ShapeDtypeStruct((2, 8 // PIX...]
    squeeze x1 -> x0, local copies, waits for them, and re-layouts: 0.78 us -> none  [shards(): sent = lax.dynamic_index_in_dim(message, layer ^ mask, 0, keepdims=False)]
    unnamed x14 -> x6, local copies, waits for them, and re-layouts: 1.42 us -> 1.88 us
  transfers between devices with their start and end apart: 7 -> 7, of which waited for: 5 -> 4; matrix products, arithmetic and copies ran while one was open for 0% -> 0% of each run, Pallas kernels for 0% -> 0%
where the time goes in v2:
time: 30.7 us; the launch traced here: 30.5 us
  waiting for transfers between devices  12.5 us (41%)
  starting transfers between devices  12.2 us (40%)
  Pallas kernels  3.96 us (13%)
  local copies, waits for them, and re-layouts  1.88 us (6%)
    ppermute x4, waiting for transfers between devices, shards(): arrived.append(lax.ppermute(bricks, 'gx', pairs))  7.74 us
    ppermute x4, starting transfers between devices, shards(): arrived.append(lax.ppermute(bricks, 'gx', pairs))  7.44 us
    ppermute x3, waiting for transfers between devices, shards(): others.append(lax.ppermute(messages[mask], 'gz', pairs))  4.76 us
    ppermute x3, starting transfers between devices, shards(): others.append(lax.ppermute(messages[mask], 'gz', pairs))  4.72 us
    pallas_call x1, Pallas kernels, shards(): pl.pallas_call(select_kernel, out_shape=[jax.ShapeDtypeStruct((BRICKS //...  2.15 us
    unnamed x6, local copies, waits for them, and re-layouts  1.88 us
    pallas_call x1, Pallas kernels, shards(): pl.pallas_call(render_kernel, out_shape=jax.ShapeDtypeStruct((2, 8 // PIX...  1.09 us
    pallas_call x1, Pallas kernels, shards(): pl.pallas_call(pack_kernel, out_shape=[box] * PLACES, in_specs=[hbm, hbm]...  0.72 us
  transfers between devices with their start and end apart: 7, of which 4 were waited for; matrix products, arithmetic and copies ran while one was open for 0% of the time, Pallas kernels for 0%

profile of v2, /device:TPU:2, one launch (start us, length us, event | category | flops | bytes accessed | tf_op | source)
XLA Modules:
  0.0 30.5 jit_solution(10260560499866321897)
XLA Ops:
  0.0 0.0 copy-start.2
  0.0 0.7 %copy-done.2 = s32[8,1,1]{0,2,1:T(1,128)S(1)} copy-done((s32[8,1,1]{0,2,1:T(1,128)S(1)}, s32[8,1,1]{0,2,1:T(1,128)}, u32[]{:S(2)}) %copy-start.2) | copy-done | bytes 56
  0.7 0.0 copy-start
  0.7 1.2 %copy-done = f32[8,8,32,128]{3,2,1,0:T(8,128)S(1)} copy-done((f32[8,8,32,128]{3,2,1,0:T(8,128)S(1)}, f32[8,8,32,128]{3,2,1,0:T(8,128)}, u32[]{:S(2)}) %copy-start) | copy-done | bytes 1048600
  1.9 0.0 copy-start.1
  1.9 0.7 %pack.1 = (f32[65,8,128]{2,1,0:T(8,128)S(1)}, f32[65,8,128]{2,1,0:T(8,128)S(1)}, f32[65,8,128]{2,1,0:T(8,128)S(1)}, f32[65,8,128]{2,1,0:T(8,128)S(1)}, f32[65,8,128]{2,1,0:T(8,128)S(1)}) custom-call(s32[8]{0:T(128)S(1)} %bitcast.6, f32[8,32,8,128]{3,2,1,0:T(8,128)S(1)} %bitcast.4), custom_call_target="tpu_custom_call" | custom-call | tf_op jit(solution)/shard_map/pack/pallas_call | solution.py:165
  2.6 2.0 %collective-permute-start = (f32[65,8,128]{2,1,0:T(8,128)S(1)}, f32[65,8,128]{2,1,0:T(8,128)S(1)}, u32[]{:S(2)}, u32[]{:S(2)}) collective-permute-start(f32[65,8,128]{2,1,0:T(8,128)S(1)} %get-tuple-element.15), channel_id=1, source_target_pairs={{0,32},{16,48},{32,64},{48,80},{64,96},{80,112},{96,128},{112,144}... | collective-permute-start | bytes 798728 | tf_op jit(solution)/shard_map/ppermute | solution.py:182
  4.6 0.0 collective-permute-start.1
  4.6 4.1 %collective-permute-start.2 = (f32[65,8,128]{2,1,0:T(8,128)S(1)}, f32[65,8,128]{2,1,0:T(8,128)S(1)}, u32[]{:S(2)}, u32[]{:S(2)}) collective-permute-start(f32[65,8,128]{2,1,0:T(8,128)S(1)} %get-tuple-element.17), channel_id=1, source_target_pairs={{0,224},{16,240},{32,0},{48,16},{64,32},{80,48},{96,64},{112,80},{... | collective-permute-start | bytes 798728 | tf_op jit(solution)/shard_map/ppermute | solution.py:182
  8.7 1.4 %collective-permute-start.3 = (f32[65,8,128]{2,1,0:T(8,128)S(1)}, f32[65,8,128]{2,1,0:T(8,128)S(1)}, u32[]{:S(2)}, u32[]{:S(2)}) collective-permute-start(f32[65,8,128]{2,1,0:T(8,128)S(1)} %get-tuple-element.18), channel_id=1, source_target_pairs={{0,240},{16,0},{32,16},{48,32},{64,48},{80,64},{96,80},{112,96},{1... | collective-permute-start | bytes 798728 | tf_op jit(solution)/shard_map/ppermute | solution.py:182
  10.1 5.7 %collective-permute-done.refs_1_ = f32[65,8,128]{2,1,0:T(8,128)S(1)} collective-permute-done((f32[65,8,128]{2,1,0:T(8,128)S(1)}, f32[65,8,128]{2,1,0:T(8,128)S(1)}, u32[]{:S(2)}, u32[]{:S(2)}) %collective-permute-start) | collective-permute-done | bytes 266272 | tf_op jit(solution)/shard_map/ppermute | solution.py:182
  15.8 2.0 %collective-permute-done.1.refs_2_ = f32[65,8,128]{2,1,0:T(8,128)S(1)} collective-permute-done((f32[65,8,128]{2,1,0:T(8,128)S(1)}, f32[65,8,128]{2,1,0:T(8,128)S(1)}, u32[]{:S(2)}, u32[]{:S(2)}) %collective-permute-start.1) | collective-permute-done | bytes 266272 | tf_op jit(solution)/shard_map/ppermute | solution.py:182
  17.8 0.0 collective-permute-done.2.refs_3_
  17.8 0.0 collective-permute-done.3.refs_4_
  17.8 0.0 copy-done.1
  17.8 2.1 %select.1 = (f32[5,8,128]{2,1,0:T(8,128)S(1)}, f32[5,8,128]{2,1,0:T(8,128)S(1)}, f32[5,8,128]{2,1,0:T(8,128)S(1)}, f32[5,8,128]{2,1,0:T(8,128)S(1)}) custom-call(s32[32,64]{1,0:T(8,128)S(1)} %bitcast.5, f32[65,8,128]{2,1,0:T(8,128)S(1)} %get-tuple-element.14.refs_0_, f32[65,8,128]{2,1,0:T(8,128)S(1)} %collective-permute-done.refs_1_, ...), custom_call_target="tpu_custom_call" | custom-call | tf_op jit(solution)/shard_map/select/pallas_call | solution.py:183
  20.0 1.6 %collective-permute-start.4 = (f32[5,8,128]{2,1,0:T(8,128)S(1)}, f32[5,8,128]{2,1,0:T(8,128)S(1)}, u32[]{:S(2)}, u32[]{:S(2)}) collective-permute-start(f32[5,8,128]{2,1,0:T(8,128)S(1)} %get-tuple-element.20), channel_id=1, source_target_pairs={{0,1},{1,0},{2,3},{3,2},{4,5},{5,4},{6,7},{7,6},{8,9},{9,8},{10,11... | collective-permute-start | bytes 61448 | tf_op jit(solution)/shard_map/ppermute | solution.py:198
  21.5 2.9 %collective-permute-start.5 = (f32[5,8,128]{2,1,0:T(8,128)S(1)}, f32[5,8,128]{2,1,0:T(8,128)S(1)}, u32[]{:S(2)}, u32[]{:S(2)}) collective-permute-start(f32[5,8,128]{2,1,0:T(8,128)S(1)} %get-tuple-element.21), channel_id=1, source_target_pairs={{0,2},{1,3},{2,0},{3,1},{4,6},{5,7},{6,4},{7,5},{8,10},{9,11},{10,... | collective-permute-start | bytes 61448 | tf_op jit(solution)/shard_map/ppermute | solution.py:198
  24.4 0.2 collective-permute-start.6
  24.7 0.0 collective-permute-done.4.refs_1_
  24.7 2.2 %collective-permute-done.5.refs_2_ = f32[5,8,128]{2,1,0:T(8,128)S(1)} collective-permute-done((f32[5,8,128]{2,1,0:T(8,128)S(1)}, f32[5,8,128]{2,1,0:T(8,128)S(1)}, u32[]{:S(2)}, u32[]{:S(2)}) %collective-permute-start.5) | collective-permute-done | bytes 20512 | tf_op jit(solution)/shard_map/ppermute | solution.py:198
  26.8 2.6 %collective-permute-done.6.refs_3_ = f32[5,8,128]{2,1,0:T(8,128)S(1)} collective-permute-done((f32[5,8,128]{2,1,0:T(8,128)S(1)}, f32[5,8,128]{2,1,0:T(8,128)S(1)}, u32[]{:S(2)}, u32[]{:S(2)}) %collective-permute-start.6) | collective-permute-done | bytes 20512 | tf_op jit(solution)/shard_map/ppermute | solution.py:198
  29.4 1.1 %render.1 = f32[2,2,16]{2,1,0:T(2,128)} custom-call(f32[5,8,128]{2,1,0:T(8,128)S(1)} %get-tuple-element.19.refs_0_, f32[5,8,128]{2,1,0:T(8,128)S(1)} %collective-permute-done.4.refs_1_, f32[5,8,128]{2,1,0:T(8,128)S(1)} %collective-permute-done.5.refs_2_, f32[5,8,128]{2,1,0:T(8,128)S(1)} %collective-permute-done.6.refs_3_), custom_call_target="tpu_custom_call" | custom-call | tf_op jit(solution)/shard_map/render/pallas_call | solution.py:199
Async XLA Ops:
  0.0 0.7 %copy-start.2 = (s32[8,1,1]{0,2,1:T(1,128)S(1)}, s32[8,1,1]{0,2,1:T(1,128)}, u32[]{:S(2)}) copy-start(s32[8,1,1]{0,2,1:T(1,128)} %param.4) | copy-start | bytes 100
  0.7 1.2 %copy-start = (f32[8,8,32,128]{3,2,1,0:T(8,128)S(1)}, f32[8,8,32,128]{3,2,1,0:T(8,128)}, u32[]{:S(2)}) copy-start(f32[8,8,32,128]{3,2,1,0:T(8,128)} %param.3) | copy-start | bytes 3145732
  1.9 15.9 %copy-start.1 = (s32[64,32]{0,1:T(8,128)S(1)}, s32[64,32]{0,1:T(8,128)}, u32[]{:S(2)}) copy-start(s32[64,32]{0,1:T(8,128)} %param.5) | copy-start | bytes 24580
  2.6 13.2 %collective-permute-start = (f32[65,8,128]{2,1,0:T(8,128)S(1)}, f32[65,8,128]{2,1,0:T(8,128)S(1)}, u32[]{:S(2)}, u32[]{:S(2)}) collective-permute-start(f32[65,8,128]{2,1,0:T(8,128)S(1)} %get-tuple-element.15), channel_id=1, source_target_pairs={{0,32},{16,48},{32,64},{48,80},{64,96},{80,112},{96,128},{112,144}... | collective-permute-start | bytes 798728 | tf_op jit(solution)/shard_map/ppermute | solution.py:182
  4.6 13.2 %collective-permute-start.1 = (f32[65,8,128]{2,1,0:T(8,128)S(1)}, f32[65,8,128]{2,1,0:T(8,128)S(1)}, u32[]{:S(2)}, u32[]{:S(2)}) collective-permute-start(f32[65,8,128]{2,1,0:T(8,128)S(1)} %get-tuple-element.16), channel_id=1, source_target_pairs={{0,16},{16,32},{32,48},{48,64},{64,80},{80,96},{96,112},{112,128},... | collective-permute-start | bytes 798728 | tf_op jit(solution)/shard_map/ppermute | solution.py:182
  4.6 13.2 %collective-permute-start.2 = (f32[65,8,128]{2,1,0:T(8,128)S(1)}, f32[65,8,128]{2,1,0:T(8,128)S(1)}, u32[]{:S(2)}, u32[]{:S(2)}) collective-permute-start(f32[65,8,128]{2,1,0:T(8,128)S(1)} %get-tuple-element.17), channel_id=1, source_target_pairs={{0,224},{16,240},{32,0},{48,16},{64,32},{80,48},{96,64},{112,80},{... | collective-permute-start | bytes 798728 | tf_op jit(solution)/shard_map/ppermute | solution.py:182
  8.7 9.1 %collective-permute-start.3 = (f32[65,8,128]{2,1,0:T(8,128)S(1)}, f32[65,8,128]{2,1,0:T(8,128)S(1)}, u32[]{:S(2)}, u32[]{:S(2)}) collective-permute-start(f32[65,8,128]{2,1,0:T(8,128)S(1)} %get-tuple-element.18), channel_id=1, source_target_pairs={{0,240},{16,0},{32,16},{48,32},{64,48},{80,64},{96,80},{112,96},{1... | collective-permute-start | bytes 798728 | tf_op jit(solution)/shard_map/ppermute | solution.py:182
  20.0 4.7 %collective-permute-start.4 = (f32[5,8,128]{2,1,0:T(8,128)S(1)}, f32[5,8,128]{2,1,0:T(8,128)S(1)}, u32[]{:S(2)}, u32[]{:S(2)}) collective-permute-start(f32[5,8,128]{2,1,0:T(8,128)S(1)} %get-tuple-element.20), channel_id=1, source_target_pairs={{0,1},{1,0},{2,3},{3,2},{4,5},{5,4},{6,7},{7,6},{8,9},{9,8},{10,11... | collective-permute-start | bytes 61448 | tf_op jit(solution)/shard_map/ppermute | solution.py:198
  21.5 5.3 %collective-permute-start.5 = (f32[5,8,128]{2,1,0:T(8,128)S(1)}, f32[5,8,128]{2,1,0:T(8,128)S(1)}, u32[]{:S(2)}, u32[]{:S(2)}) collective-permute-start(f32[5,8,128]{2,1,0:T(8,128)S(1)} %get-tuple-element.21), channel_id=1, source_target_pairs={{0,2},{1,3},{2,0},{3,1},{4,6},{5,7},{6,4},{7,5},{8,10},{9,11},{10,... | collective-permute-start | bytes 61448 | tf_op jit(solution)/shard_map/ppermute | solution.py:198
  24.4 5.0 %collective-permute-start.6 = (f32[5,8,128]{2,1,0:T(8,128)S(1)}, f32[5,8,128]{2,1,0:T(8,128)S(1)}, u32[]{:S(2)}, u32[]{:S(2)}) collective-permute-start(f32[5,8,128]{2,1,0:T(8,128)S(1)} %get-tuple-element.22), channel_id=1, source_target_pairs={{0,3},{1,2},{2,1},{3,0},{4,7},{5,6},{6,5},{7,4},{8,11},{9,10},{10,... | collective-permute-start | bytes 61448 | tf_op jit(solution)/shard_map/ppermute | solution.py:198

commit v3 on v2

--- a/solution.py
+++ b/solution.py
@@ -20,8 +20,16 @@
 NONE = BRICKS
 VMEM_BYTES = 4 << 20
 
-MOVES = (2, 1, -2, -1)
+MOVES = (1, 2, -2, -1)
+EARLY = 2
 PLACES = len(MOVES) + 1
+SENDS = ((3, 2, 0, 1), (2, 3, 1, 0), (1, 0, 3, 2))
+TILES = BRICKS // 2
+
+
+def look_up(table, position):
+    packed = sum(entry << (4 * index) for index, entry in enumerate(table))
+    return (jnp.int32(packed) >> (4 * position)) & 15
 
 
 def find_bricks(home_ref, target):
@@ -61,60 +69,73 @@
             out_ref[pl.ds(place * ROWS, ROWS)] = dens_ref[brick]
 
 
-def select_kernel(jitter_ref, *refs):
-    arrived = refs[:PLACES]
-    outs = refs[PLACES : PLACES + LAYERS]
-    sample_ref, peak_ref = refs[PLACES + LAYERS :]
-    layer = lax.axis_index("gz")
+def take_samples(jitter_ref, arrived, sample_ref, peak_ref):
     lane = lax.broadcasted_iota(jnp.int32, (8, 128), 1)
     plane = (lane >> 3) & 7
     collision = (lane & 7) * STRIDE
     jitter = jnp.concatenate([jitter_ref[...], jitter_ref[...]], axis=1)
-
-    def handle(source_ref, place):
-        label = source_ref[CAP * ROWS, place : place + 1, 0:1][0, 0]
-        slot = label.astype(jnp.int32)
-
-        @pl.when(slot < BRICKS)
-        def _():
-            for quarter in range(QUARTERS):
-                moved = jnp.take_along_axis(
-                    jitter[quarter * 8 : (quarter + 1) * 8],
-                    slot * 8 + plane,
-                    axis=1,
-                    mode="promise_in_bounds",
-                )
-                where_at = collision + moved
-                samples = None
-                peak = None
-                for x in range(8):
-                    cells = source_ref[place * ROWS + x * QUARTERS + quarter]
-                    taken = jnp.take_along_axis(cells, where_at, axis=1, mode="promise_in_bounds")
-                    samples = taken if x == 0 else jnp.where(plane == x, taken, samples)
-                    peak = cells if x == 0 else jnp.maximum(peak, cells)
-                sample_ref[slot, quarter] = samples
-                peak_ref[quarter, pl.ds(slot, 1), :] = jnp.max(peak, axis=0, keepdims=True)
-
+    slots = []
     for source_ref in arrived:
         for place in range(CAP):
-            handle(source_ref, place)
-    for mask, out_ref in enumerate(outs):
-        quarter = layer ^ mask
-        for tile in range(BRICKS // 2):
+            label = source_ref[CAP * ROWS, place : place + 1, 0:1][0, 0]
+            slots.append(label.astype(jnp.int32))
+    for number, slot in enumerate(slots):
+        source_ref, place = arrived[number // CAP], number % CAP
+        for quarter in range(QUARTERS):
+            moved = jnp.take_along_axis(
+                jitter[quarter * 8 : (quarter + 1) * 8],
+                slot * 8 + plane,
+                axis=1,
+                mode="promise_in_bounds",
+            )
+            where_at = collision + moved
+            samples = None
+            peak = None
+            for x in range(8):
+                cells = source_ref[place * ROWS + x * QUARTERS + quarter]
+                taken = jnp.take_along_axis(cells, where_at, axis=1, mode="promise_in_bounds")
+                samples = taken if x == 0 else jnp.where(plane == x, taken, samples)
+                peak = cells if x == 0 else jnp.maximum(peak, cells)
+            sample_ref[slot, quarter] = samples
+            peak_ref[quarter, pl.ds(slot, 1), :] = jnp.max(peak, axis=0, keepdims=True)
+
+
+def early_kernel(jitter_ref, *refs):
+    arrived = refs[: EARLY + 1]
+    sample_ref, peak_ref = refs[EARLY + 1 :]
+    take_samples(jitter_ref, arrived, sample_ref, peak_ref)
+
+
+def late_kernel(jitter_ref, early_samples, early_peaks, *refs):
+    count = len(MOVES) - EARLY
+    arrived = refs[:count]
+    outs = refs[count : count + LAYERS]
+    sample_ref, peak_ref = refs[count + LAYERS :]
+    sample_ref[...] = early_samples[...]
+    peak_ref[...] = early_peaks[...]
+    take_samples(jitter_ref, arrived, sample_ref, peak_ref)
+    layer = lax.axis_index("gz")
+    lane = lax.broadcasted_iota(jnp.int32, (8, 128), 1)
+    quarters = [layer] + [look_up(table, layer) for table in SENDS]
+    for quarter, out_ref in zip(quarters, outs):
+        for tile in range(TILES):
             out_ref[tile] = jnp.where(
                 lane < 64, sample_ref[2 * tile, quarter], sample_ref[2 * tile + 1, quarter]
             )
-        peak = jnp.max(peak_ref[quarter], axis=1, keepdims=True)
-        out_ref[BRICKS // 2] = jnp.broadcast_to(peak, (8, 128))
+        peak = jnp.max(peak_ref[quarter, :BRICKS], axis=1, keepdims=True)
+        out_ref[TILES] = jnp.broadcast_to(peak, (8, 128))
 
 
 def render_kernel(*refs):
     out_ref, held_ref = refs[LAYERS:]
     layer = lax.axis_index("gz")
-    for mask, message in enumerate(refs[:LAYERS]):
-        held_ref[layer ^ mask] = message[...]
+    sources = [layer]
+    for table in SENDS:
+        sources.append(look_up([table.index(place) for place in range(LAYERS)], layer))
+    for source, message in zip(sources, refs[:LAYERS]):
+        held_ref[source] = message[...]
     lane = lax.broadcasted_iota(jnp.int32, (8, 128), 1)
-    tiles = BRICKS // 2
+    tiles = TILES
     peak = held_ref[0, tiles]
     for depth in range(1, LAYERS):
         peak = jnp.maximum(peak, held_ref[depth, tiles])
@@ -157,10 +178,13 @@
 
 
 def shards(sim_density, brick_home, jitter):
-    home = brick_home.reshape(BRICKS)
-    density = sim_density.reshape(BRICKS, ROWS, 8, 128)
+    home = pltpu.with_memory_space_constraint(brick_home.reshape(BRICKS), pltpu.HBM)
+    density = pltpu.with_memory_space_constraint(
+        sim_density.reshape(BRICKS, ROWS, 8, 128), pltpu.HBM
+    )
     vmem = pl.BlockSpec(memory_space=pltpu.VMEM)
     hbm = pl.BlockSpec(memory_space=pltpu.HBM)
+    params = pltpu.CompilerParams(vmem_limit_bytes=VMEM_BYTES)
     box = jax.ShapeDtypeStruct((CAP * ROWS + 1, 8, 128), jnp.float32)
     packed = pl.pallas_call(
         pack_kernel,
@@ -173,36 +197,48 @@
             pltpu.SemaphoreType.DMA,
             pltpu.SemaphoreType.DMA,
         ],
-        compiler_params=pltpu.CompilerParams(vmem_limit_bytes=VMEM_BYTES),
+        compiler_params=params,
         name="pack",
     )(home, density)
     arrived = []
     for move, bricks in zip(MOVES, packed):
         pairs = [(source, (source + move) % GROUP) for source in range(GROUP)]
         arrived.append(lax.ppermute(bricks, "gx", pairs))
+    sample_box = (BRICKS + 1, QUARTERS, 8, 128)
+    peak_box = (QUARTERS, 2 * BRICKS, 128)
+    gathered = pl.pallas_call(
+        early_kernel,
+        out_shape=[
+            jax.ShapeDtypeStruct(sample_box, jnp.float32),
+            jax.ShapeDtypeStruct(peak_box, jnp.float32),
+        ],
+        in_specs=[vmem] * (2 + EARLY),
+        out_specs=[vmem] * 2,
+        compiler_params=params,
+        name="early",
+    )(jitter.T, packed[-1], *arrived[:EARLY])
     messages = pl.pallas_call(
-        select_kernel,
-        out_shape=[jax.ShapeDtypeStruct((BRICKS // 2 + 1, 8, 128), jnp.float32)] * LAYERS,
-        in_specs=[vmem] * (1 + PLACES),
+        late_kernel,
+        out_shape=[jax.ShapeDtypeStruct((TILES + 1, 8, 128), jnp.float32)] * LAYERS,
+        in_specs=[vmem] * (3 + len(MOVES) - EARLY),
         out_specs=[vmem] * LAYERS,
         scratch_shapes=[
-            pltpu.VMEM((BRICKS, QUARTERS, 8, 128), jnp.float32),
-            pltpu.VMEM((QUARTERS, BRICKS, 128), jnp.float32),
+            pltpu.VMEM(sample_box, jnp.float32),
+            pltpu.VMEM(peak_box, jnp.float32),
         ],
-        compiler_params=pltpu.CompilerParams(vmem_limit_bytes=VMEM_BYTES),
-        name="select",
-    )(jitter.T, packed[-1], *arrived)
+        compiler_params=params,
+        name="late",
+    )(jitter.T, *gathered, *arrived[EARLY:])
     others = []
-    for mask in range(1, LAYERS):
-        pairs = [(source, source ^ mask) for source in range(LAYERS)]
-        others.append(lax.ppermute(messages[mask], "gz", pairs))
+    for table, message in zip(SENDS, messages[1:]):
+        others.append(lax.ppermute(message, "gz", list(enumerate(table))))
     image = pl.pallas_call(
         render_kernel,
         out_shape=jax.ShapeDtypeStruct((2, 8 // PIXEL, 16), jnp.float32),
         in_specs=[vmem] * LAYERS,
         out_specs=vmem,
-        scratch_shapes=[pltpu.VMEM((LAYERS, BRICKS // 2 + 1, 8, 128), jnp.float32)],
-        compiler_params=pltpu.CompilerParams(vmem_limit_bytes=VMEM_BYTES),
+        scratch_shapes=[pltpu.VMEM((LAYERS, TILES + 1, 8, 128), jnp.float32)],
+        compiler_params=params,
         name="render",
     )(messages[0], *others)
     return jnp.transpose(image, (0, 2, 1))

time: 30.7 us -> 26.8 us (0.87)
  the two profiles are of different devices: /device:TPU:2 before, /device:TPU:1 now
where the time goes in v3:
time: 26.8 us; the launch traced here: 26.7 us
  starting transfers between devices  11.9 us (44%)
  waiting for transfers between devices  10.9 us (41%)
  Pallas kernels  3.83 us (14%)
    ppermute x4, waiting for transfers between devices, shards(): arrived.append(lax.ppermute(bricks, 'gx', pairs))  8.38 us
    ppermute x4, starting transfers between devices, shards(): arrived.append(lax.ppermute(bricks, 'gx', pairs))  7.55 us
    ppermute x3, starting transfers between devices, shards(): others.append(lax.ppermute(message, 'gz', list(enumerate(table))))  4.34 us
    ppermute x3, waiting for transfers between devices, shards(): others.append(lax.ppermute(message, 'gz', list(enumerate(table))))  2.54 us
    pallas_call x1, Pallas kernels, shards(): pl.pallas_call(pack_kernel, out_shape=[box] * PLACES, in_specs=[hbm, hbm]...  1.34 us
    pallas_call x1, Pallas kernels, shards(): pl.pallas_call(render_kernel, out_shape=jax.ShapeDtypeStruct((2, 8 // PIX...  1.1 us
    pallas_call x1, Pallas kernels, shards(): pl.pallas_call(early_kernel, out_shape=[jax.ShapeDtypeStruct(sample_box,...  0.98 us
  transfers between devices with their start and end apart: 7, of which 3 were waited for; matrix products, arithmetic and copies ran while one was open for 0% of the time, Pallas kernels for 4%

profile of v3, /device:TPU:1, one launch (start us, length us, event | category | flops | bytes accessed | tf_op | source)
XLA Modules:
  0.0 26.7 jit_solution(2789532172522623742)
XLA Ops:
  0.0 0.0 copy-start
  0.0 1.3 %pack.1 = (f32[65,8,128]{2,1,0:T(8,128)S(1)}, f32[65,8,128]{2,1,0:T(8,128)S(1)}, f32[65,8,128]{2,1,0:T(8,128)S(1)}, f32[65,8,128]{2,1,0:T(8,128)S(1)}, f32[65,8,128]{2,1,0:T(8,128)S(1)}) custom-call(s32[8]{0:T(128)} %bitcast.7, f32[8,32,8,128]{3,2,1,0:T(8,128)} %bitcast.6), custom_call_target="tpu_custom_call" | custom-call | tf_op jit(solution)/shard_map/pack/pallas_call | solution.py:189
  1.4 3.0 %collective-permute-start = (f32[65,8,128]{2,1,0:T(8,128)S(1)}, f32[65,8,128]{2,1,0:T(8,128)S(1)}, u32[]{:S(2)}, u32[]{:S(2)}) collective-permute-start(f32[65,8,128]{2,1,0:T(8,128)S(1)} %get-tuple-element.17), channel_id=1, source_target_pairs={{0,16},{16,32},{32,48},{48,64},{64,80},{80,96},{96,112},{112,128},... | collective-permute-start | bytes 798728 | tf_op jit(solution)/shard_map/ppermute | solution.py:206
  4.4 1.6 %collective-permute-start.1 = (f32[65,8,128]{2,1,0:T(8,128)S(1)}, f32[65,8,128]{2,1,0:T(8,128)S(1)}, u32[]{:S(2)}, u32[]{:S(2)}) collective-permute-start(f32[65,8,128]{2,1,0:T(8,128)S(1)} %get-tuple-element.18), channel_id=1, source_target_pairs={{0,32},{16,48},{32,64},{48,80},{64,96},{80,112},{96,128},{112,144}... | collective-permute-start | bytes 798728 | tf_op jit(solution)/shard_map/ppermute | solution.py:206
  6.0 1.9 %collective-permute-start.2 = (f32[65,8,128]{2,1,0:T(8,128)S(1)}, f32[65,8,128]{2,1,0:T(8,128)S(1)}, u32[]{:S(2)}, u32[]{:S(2)}) collective-permute-start(f32[65,8,128]{2,1,0:T(8,128)S(1)} %get-tuple-element.21), channel_id=1, source_target_pairs={{0,224},{16,240},{32,0},{48,16},{64,32},{80,48},{96,64},{112,80},{... | collective-permute-start | bytes 798728 | tf_op jit(solution)/shard_map/ppermute | solution.py:206
  7.9 1.0 %collective-permute-start.3 = (f32[65,8,128]{2,1,0:T(8,128)S(1)}, f32[65,8,128]{2,1,0:T(8,128)S(1)}, u32[]{:S(2)}, u32[]{:S(2)}) collective-permute-start(f32[65,8,128]{2,1,0:T(8,128)S(1)} %get-tuple-element.22), channel_id=1, source_target_pairs={{0,240},{16,0},{32,16},{48,32},{64,48},{80,64},{96,80},{112,96},{1... | collective-permute-start | bytes 798728 | tf_op jit(solution)/shard_map/ppermute | solution.py:206
  8.9 1.1 %collective-permute-done.refs_1_ = f32[65,8,128]{2,1,0:T(8,128)S(1)} collective-permute-done((f32[65,8,128]{2,1,0:T(8,128)S(1)}, f32[65,8,128]{2,1,0:T(8,128)S(1)}, u32[]{:S(2)}, u32[]{:S(2)}) %collective-permute-start) | collective-permute-done | bytes 266272 | tf_op jit(solution)/shard_map/ppermute | solution.py:206
  10.0 7.3 %collective-permute-done.1.refs_2_ = f32[65,8,128]{2,1,0:T(8,128)S(1)} collective-permute-done((f32[65,8,128]{2,1,0:T(8,128)S(1)}, f32[65,8,128]{2,1,0:T(8,128)S(1)}, u32[]{:S(2)}, u32[]{:S(2)}) %collective-permute-start.1) | collective-permute-done | bytes 266272 | tf_op jit(solution)/shard_map/ppermute | solution.py:206
  17.3 0.0 copy-done
  17.3 1.0 %early.1 = (f32[9,4,8,128]{3,2,1,0:T(8,128)S(1)}, f32[4,16,128]{2,1,0:T(8,128)S(1)}) custom-call(s32[32,64]{1,0:T(8,128)S(1)} %bitcast.4, f32[65,8,128]{2,1,0:T(8,128)S(1)} %get-tuple-element.16.refs_0_, f32[65,8,128]{2,1,0:T(8,128)S(1)} %collective-permute-done.refs_1_, f32[65,8,128]{2,1,0:T(8,128)S(1)} %collective-permute-done.1.refs_2_), custom_call_target="tpu_custom_call" | custom-call | tf_op jit(solution)/shard_map/early/pallas_call | solution.py:209
  18.3 0.0 collective-permute-done.2.refs_0_
  18.3 0.0 collective-permute-done.3.refs_1_
  18.3 0.4 %late.1 = (f32[5,8,128]{2,1,0:T(8,128)S(1)}, f32[5,8,128]{2,1,0:T(8,128)S(1)}, f32[5,8,128]{2,1,0:T(8,128)S(1)}, f32[5,8,128]{2,1,0:T(8,128)S(1)}) custom-call(s32[32,64]{1,0:T(8,128)S(1)} %bitcast.5, f32[9,4,8,128]{3,2,1,0:T(8,128)S(1)} %get-tuple-element.19.early_samples, f32[4,16,128]{2,1,0:T(8,128)S(1)} %get-tuple-element.20.early_peaks, ...), custom_call_target="tpu_custom_call" | custom-call | tf_op jit(solution)/shard_map/late/pallas_call | solution.py:220
  18.7 2.8 %collective-permute-start.4 = (f32[5,8,128]{2,1,0:T(8,128)S(1)}, f32[5,8,128]{2,1,0:T(8,128)S(1)}, u32[]{:S(2)}, u32[]{:S(2)}) collective-permute-start(f32[5,8,128]{2,1,0:T(8,128)S(1)} %get-tuple-element.24), channel_id=1, source_target_pairs={{0,3},{1,2},{2,0},{3,1},{4,7},{5,6},{6,4},{7,5},{8,11},{9,10},{10,... | collective-permute-start | bytes 61448 | tf_op jit(solution)/shard_map/ppermute | solution.py:234
  21.5 0.3 %collective-permute-start.5 = (f32[5,8,128]{2,1,0:T(8,128)S(1)}, f32[5,8,128]{2,1,0:T(8,128)S(1)}, u32[]{:S(2)}, u32[]{:S(2)}) collective-permute-start(f32[5,8,128]{2,1,0:T(8,128)S(1)} %get-tuple-element.25), channel_id=1, source_target_pairs={{0,2},{1,3},{2,1},{3,0},{4,6},{5,7},{6,5},{7,4},{8,10},{9,11},{10,... | collective-permute-start | bytes 61448 | tf_op jit(solution)/shard_map/ppermute | solution.py:234
  21.8 1.3 %collective-permute-start.6 = (f32[5,8,128]{2,1,0:T(8,128)S(1)}, f32[5,8,128]{2,1,0:T(8,128)S(1)}, u32[]{:S(2)}, u32[]{:S(2)}) collective-permute-start(f32[5,8,128]{2,1,0:T(8,128)S(1)} %get-tuple-element.26), channel_id=1, source_target_pairs={{0,1},{1,0},{2,3},{3,2},{4,5},{5,4},{6,7},{7,6},{8,9},{9,8},{10,11... | collective-permute-start | bytes 61448 | tf_op jit(solution)/shard_map/ppermute | solution.py:234
  23.0 0.0 collective-permute-done.4.refs_1_
  23.0 2.5 %collective-permute-done.5.refs_2_ = f32[5,8,128]{2,1,0:T(8,128)S(1)} collective-permute-done((f32[5,8,128]{2,1,0:T(8,128)S(1)}, f32[5,8,128]{2,1,0:T(8,128)S(1)}, u32[]{:S(2)}, u32[]{:S(2)}) %collective-permute-start.5) | collective-permute-done | bytes 20512 | tf_op jit(solution)/shard_map/ppermute | solution.py:234
  25.6 0.0 collective-permute-done.6.refs_3_
  25.6 1.1 %render.1 = f32[2,2,16]{2,1,0:T(2,128)} custom-call(f32[5,8,128]{2,1,0:T(8,128)S(1)} %get-tuple-element.23.refs_0_, f32[5,8,128]{2,1,0:T(8,128)S(1)} %collective-permute-done.4.refs_1_, f32[5,8,128]{2,1,0:T(8,128)S(1)} %collective-permute-done.5.refs_2_, f32[5,8,128]{2,1,0:T(8,128)S(1)} %collective-permute-done.6.refs_3_), custom_call_target="tpu_custom_call" | custom-call | tf_op jit(solution)/shard_map/render/pallas_call | solution.py:235
Async XLA Ops:
  0.0 17.3 %copy-start = (s32[64,32]{0,1:T(8,128)S(1)}, s32[64,32]{0,1:T(8,128)}, u32[]{:S(2)}) copy-start(s32[64,32]{0,1:T(8,128)} %param.5) | copy-start | bytes 24580
  1.4 8.6 %collective-permute-start = (f32[65,8,128]{2,1,0:T(8,128)S(1)}, f32[65,8,128]{2,1,0:T(8,128)S(1)}, u32[]{:S(2)}, u32[]{:S(2)}) collective-permute-start(f32[65,8,128]{2,1,0:T(8,128)S(1)} %get-tuple-element.17), channel_id=1, source_target_pairs={{0,16},{16,32},{32,48},{48,64},{64,80},{80,96},{96,112},{112,128},... | collective-permute-start | bytes 798728 | tf_op jit(solution)/shard_map/ppermute | solution.py:206
  4.4 12.9 %collective-permute-start.1 = (f32[65,8,128]{2,1,0:T(8,128)S(1)}, f32[65,8,128]{2,1,0:T(8,128)S(1)}, u32[]{:S(2)}, u32[]{:S(2)}) collective-permute-start(f32[65,8,128]{2,1,0:T(8,128)S(1)} %get-tuple-element.18), channel_id=1, source_target_pairs={{0,32},{16,48},{32,64},{48,80},{64,96},{80,112},{96,128},{112,144}... | collective-permute-start | bytes 798728 | tf_op jit(solution)/shard_map/ppermute | solution.py:206
  6.0 12.2 %collective-permute-start.2 = (f32[65,8,128]{2,1,0:T(8,128)S(1)}, f32[65,8,128]{2,1,0:T(8,128)S(1)}, u32[]{:S(2)}, u32[]{:S(2)}) collective-permute-start(f32[65,8,128]{2,1,0:T(8,128)S(1)} %get-tuple-element.21), channel_id=1, source_target_pairs={{0,224},{16,240},{32,0},{48,16},{64,32},{80,48},{96,64},{112,80},{... | collective-permute-start | bytes 798728 | tf_op jit(solution)/shard_map/ppermute | solution.py:206
  7.9 10.3 %collective-permute-start.3 = (f32[65,8,128]{2,1,0:T(8,128)S(1)}, f32[65,8,128]{2,1,0:T(8,128)S(1)}, u32[]{:S(2)}, u32[]{:S(2)}) collective-permute-start(f32[65,8,128]{2,1,0:T(8,128)S(1)} %get-tuple-element.22), channel_id=1, source_target_pairs={{0,240},{16,0},{32,16},{48,32},{64,48},{80,64},{96,80},{112,96},{1... | collective-permute-start | bytes 798728 | tf_op jit(solution)/shard_map/ppermute | solution.py:206
  18.7 4.3 %collective-permute-start.4 = (f32[5,8,128]{2,1,0:T(8,128)S(1)}, f32[5,8,128]{2,1,0:T(8,128)S(1)}, u32[]{:S(2)}, u32[]{:S(2)}) collective-permute-start(f32[5,8,128]{2,1,0:T(8,128)S(1)} %get-tuple-element.24), channel_id=1, source_target_pairs={{0,3},{1,2},{2,0},{3,1},{4,7},{5,6},{6,4},{7,5},{8,11},{9,10},{10,... | collective-permute-start | bytes 61448 | tf_op jit(solution)/shard_map/ppermute | solution.py:234
  21.5 4.1 %collective-permute-start.5 = (f32[5,8,128]{2,1,0:T(8,128)S(1)}, f32[5,8,128]{2,1,0:T(8,128)S(1)}, u32[]{:S(2)}, u32[]{:S(2)}) collective-permute-start(f32[5,8,128]{2,1,0:T(8,128)S(1)} %get-tuple-element.25), channel_id=1, source_target_pairs={{0,2},{1,3},{2,1},{3,0},{4,6},{5,7},{6,5},{7,4},{8,10},{9,11},{10,... | collective-permute-start | bytes 61448 | tf_op jit(solution)/shard_map/ppermute | solution.py:234
  21.8 3.8 %collective-permute-start.6 = (f32[5,8,128]{2,1,0:T(8,128)S(1)}, f32[5,8,128]{2,1,0:T(8,128)S(1)}, u32[]{:S(2)}, u32[]{:S(2)}) collective-permute-start(f32[5,8,128]{2,1,0:T(8,128)S(1)} %get-tuple-element.26), channel_id=1, source_target_pairs={{0,1},{1,0},{2,3},{3,2},{4,5},{5,4},{6,7},{7,6},{8,9},{9,8},{10,11... | collective-permute-start | bytes 61448 | tf_op jit(solution)/shard_map/ppermute | solution.py:234

commit v4 on v3

--- a/solution.py
+++ b/solution.py
@@ -21,7 +21,8 @@
 VMEM_BYTES = 4 << 20
 
 MOVES = (1, 2, -2, -1)
-EARLY = 2
+EARLY = (0, 2)
+LATE = (1, 3)
 PLACES = len(MOVES) + 1
 SENDS = ((3, 2, 0, 1), (2, 3, 1, 0), (1, 0, 3, 2))
 TILES = BRICKS // 2
@@ -101,13 +102,13 @@
 
 
 def early_kernel(jitter_ref, *refs):
-    arrived = refs[: EARLY + 1]
-    sample_ref, peak_ref = refs[EARLY + 1 :]
+    arrived = refs[: len(EARLY) + 1]
+    sample_ref, peak_ref = refs[len(EARLY) + 1 :]
     take_samples(jitter_ref, arrived, sample_ref, peak_ref)
 
 
 def late_kernel(jitter_ref, early_samples, early_peaks, *refs):
-    count = len(MOVES) - EARLY
+    count = len(LATE)
     arrived = refs[:count]
     outs = refs[count : count + LAYERS]
     sample_ref, peak_ref = refs[count + LAYERS :]
@@ -212,15 +213,15 @@
             jax.ShapeDtypeStruct(sample_box, jnp.float32),
             jax.ShapeDtypeStruct(peak_box, jnp.float32),
         ],
-        in_specs=[vmem] * (2 + EARLY),
+        in_specs=[vmem] * (2 + len(EARLY)),
         out_specs=[vmem] * 2,
         compiler_params=params,
         name="early",
-    )(jitter.T, packed[-1], *arrived[:EARLY])
+    )(jitter.T, packed[-1], *[arrived[number] for number in EARLY])
     messages = pl.pallas_call(
         late_kernel,
         out_shape=[jax.ShapeDtypeStruct((TILES + 1, 8, 128), jnp.float32)] * LAYERS,
-        in_specs=[vmem] * (3 + len(MOVES) - EARLY),
+        in_specs=[vmem] * (3 + len(LATE)),
         out_specs=[vmem] * LAYERS,
         scratch_shapes=[
             pltpu.VMEM(sample_box, jnp.float32),
@@ -228,7 +229,7 @@
         ],
         compiler_params=params,
         name="late",
-    )(jitter.T, *gathered, *arrived[EARLY:])
+    )(jitter.T, *gathered, *[arrived[number] for number in LATE])
     others = []
     for table, message in zip(SENDS, messages[1:]):
         others.append(lax.ppermute(message, "gz", list(enumerate(table))))

time: 26.8 us -> 26.2 us (0.978)
  the two profiles are of different devices: /device:TPU:1 before, /device:TPU:2 now
where the time goes in v4:
time: 26.2 us; the launch traced here: 26.1 us
  starting transfers between devices  13.3 us (51%)
  waiting for transfers between devices  8.95 us (34%)
  Pallas kernels  3.83 us (15%)
    ppermute x4, starting transfers between devices, shards(): arrived.append(lax.ppermute(bricks, 'gx', pairs))  8.07 us
    ppermute x4, waiting for transfers between devices, shards(): arrived.append(lax.ppermute(bricks, 'gx', pairs))  6.05 us
    ppermute x3, starting transfers between devices, shards(): others.append(lax.ppermute(message, 'gz', list(enumerate(table))))  5.18 us
    ppermute x3, waiting for transfers between devices, shards(): others.append(lax.ppermute(message, 'gz', list(enumerate(table))))  2.9 us
    pallas_call x1, Pallas kernels, shards(): pl.pallas_call(pack_kernel, out_shape=[box] * PLACES, in_specs=[hbm, hbm]...  1.34 us
    pallas_call x1, Pallas kernels, shards(): pl.pallas_call(render_kernel, out_shape=jax.ShapeDtypeStruct((2, 8 // PIX...  1.1 us
    pallas_call x1, Pallas kernels, shards(): pl.pallas_call(early_kernel, out_shape=[jax.ShapeDtypeStruct(sample_box,...  0.98 us
  transfers between devices with their start and end apart: 7, of which 5 were waited for; matrix products, arithmetic and copies ran while one was open for 0% of the time, Pallas kernels for 4%

profile of v4, /device:TPU:2, one launch (start us, length us, event | category | flops | bytes accessed | tf_op | source)
XLA Modules:
  0.0 26.1 jit_solution(7264713177064515228)
XLA Ops:
  0.0 0.0 copy-start
  0.0 1.3 %pack.1 = (f32[65,8,128]{2,1,0:T(8,128)S(1)}, f32[65,8,128]{2,1,0:T(8,128)S(1)}, f32[65,8,128]{2,1,0:T(8,128)S(1)}, f32[65,8,128]{2,1,0:T(8,128)S(1)}, f32[65,8,128]{2,1,0:T(8,128)S(1)}) custom-call(s32[8]{0:T(128)} %bitcast.7, f32[8,32,8,128]{3,2,1,0:T(8,128)} %bitcast.6), custom_call_target="tpu_custom_call" | custom-call | tf_op jit(solution)/shard_map/pack/pallas_call | solution.py:190
  1.4 0.0 collective-permute-start
  1.4 5.9 %collective-permute-start.1 = (f32[65,8,128]{2,1,0:T(8,128)S(1)}, f32[65,8,128]{2,1,0:T(8,128)S(1)}, u32[]{:S(2)}, u32[]{:S(2)}) collective-permute-start(f32[65,8,128]{2,1,0:T(8,128)S(1)} %get-tuple-element.18), channel_id=1, source_target_pairs={{0,224},{16,240},{32,0},{48,16},{64,32},{80,48},{96,64},{112,80},{... | collective-permute-start | bytes 798728 | tf_op jit(solution)/shard_map/ppermute | solution.py:207
  7.3 0.0 collective-permute-start.2
  7.3 2.1 %collective-permute-start.3 = (f32[65,8,128]{2,1,0:T(8,128)S(1)}, f32[65,8,128]{2,1,0:T(8,128)S(1)}, u32[]{:S(2)}, u32[]{:S(2)}) collective-permute-start(f32[65,8,128]{2,1,0:T(8,128)S(1)} %get-tuple-element.22), channel_id=1, source_target_pairs={{0,240},{16,0},{32,16},{48,32},{64,48},{80,64},{96,80},{112,96},{1... | collective-permute-start | bytes 798728 | tf_op jit(solution)/shard_map/ppermute | solution.py:207
  9.4 1.3 %collective-permute-done.refs_1_ = f32[65,8,128]{2,1,0:T(8,128)S(1)} collective-permute-done((f32[65,8,128]{2,1,0:T(8,128)S(1)}, f32[65,8,128]{2,1,0:T(8,128)S(1)}, u32[]{:S(2)}, u32[]{:S(2)}) %collective-permute-start) | collective-permute-done | bytes 266272 | tf_op jit(solution)/shard_map/ppermute | solution.py:207
  10.8 2.2 %collective-permute-done.1.refs_2_ = f32[65,8,128]{2,1,0:T(8,128)S(1)} collective-permute-done((f32[65,8,128]{2,1,0:T(8,128)S(1)}, f32[65,8,128]{2,1,0:T(8,128)S(1)}, u32[]{:S(2)}, u32[]{:S(2)}) %collective-permute-start.1) | collective-permute-done | bytes 266272 | tf_op jit(solution)/shard_map/ppermute | solution.py:207
  13.0 0.0 copy-done
  13.0 1.0 %early.1 = (f32[9,4,8,128]{3,2,1,0:T(8,128)S(1)}, f32[4,16,128]{2,1,0:T(8,128)S(1)}) custom-call(s32[32,64]{1,0:T(8,128)S(1)} %bitcast.4, f32[65,8,128]{2,1,0:T(8,128)S(1)} %get-tuple-element.16.refs_0_, f32[65,8,128]{2,1,0:T(8,128)S(1)} %collective-permute-done.refs_1_, f32[65,8,128]{2,1,0:T(8,128)S(1)} %collective-permute-done.1.refs_2_), custom_call_target="tpu_custom_call" | custom-call | tf_op jit(solution)/shard_map/early/pallas_call | solution.py:210
  13.9 2.5 %collective-permute-done.2.refs_0_ = f32[65,8,128]{2,1,0:T(8,128)S(1)} collective-permute-done((f32[65,8,128]{2,1,0:T(8,128)S(1)}, f32[65,8,128]{2,1,0:T(8,128)S(1)}, u32[]{:S(2)}, u32[]{:S(2)}) %collective-permute-start.2) | collective-permute-done | bytes 266272 | tf_op jit(solution)/shard_map/ppermute | solution.py:207
  16.5 0.0 collective-permute-done.3.refs_1_
  16.5 0.4 %late.1 = (f32[5,8,128]{2,1,0:T(8,128)S(1)}, f32[5,8,128]{2,1,0:T(8,128)S(1)}, f32[5,8,128]{2,1,0:T(8,128)S(1)}, f32[5,8,128]{2,1,0:T(8,128)S(1)}) custom-call(s32[32,64]{1,0:T(8,128)S(1)} %bitcast.5, f32[9,4,8,128]{3,2,1,0:T(8,128)S(1)} %get-tuple-element.19.early_samples, f32[4,16,128]{2,1,0:T(8,128)S(1)} %get-tuple-element.20.early_peaks, ...), custom_call_target="tpu_custom_call" | custom-call | tf_op jit(solution)/shard_map/late/pallas_call | solution.py:221
  16.9 3.1 %collective-permute-start.4 = (f32[5,8,128]{2,1,0:T(8,128)S(1)}, f32[5,8,128]{2,1,0:T(8,128)S(1)}, u32[]{:S(2)}, u32[]{:S(2)}) collective-permute-start(f32[5,8,128]{2,1,0:T(8,128)S(1)} %get-tuple-element.24), channel_id=1, source_target_pairs={{0,3},{1,2},{2,0},{3,1},{4,7},{5,6},{6,4},{7,5},{8,11},{9,10},{10,... | collective-permute-start | bytes 61448 | tf_op jit(solution)/shard_map/ppermute | solution.py:235
  20.0 0.5 %collective-permute-start.5 = (f32[5,8,128]{2,1,0:T(8,128)S(1)}, f32[5,8,128]{2,1,0:T(8,128)S(1)}, u32[]{:S(2)}, u32[]{:S(2)}) collective-permute-start(f32[5,8,128]{2,1,0:T(8,128)S(1)} %get-tuple-element.25), channel_id=1, source_target_pairs={{0,2},{1,3},{2,1},{3,0},{4,6},{5,7},{6,5},{7,4},{8,10},{9,11},{10,... | collective-permute-start | bytes 61448 | tf_op jit(solution)/shard_map/ppermute | solution.py:235
  20.5 1.6 %collective-permute-start.6 = (f32[5,8,128]{2,1,0:T(8,128)S(1)}, f32[5,8,128]{2,1,0:T(8,128)S(1)}, u32[]{:S(2)}, u32[]{:S(2)}) collective-permute-start(f32[5,8,128]{2,1,0:T(8,128)S(1)} %get-tuple-element.26), channel_id=1, source_target_pairs={{0,1},{1,0},{2,3},{3,2},{4,5},{5,4},{6,7},{7,6},{8,9},{9,8},{10,11... | collective-permute-start | bytes 61448 | tf_op jit(solution)/shard_map/ppermute | solution.py:235
  22.1 0.2 collective-permute-done.4.refs_1_
  22.2 2.7 %collective-permute-done.5.refs_2_ = f32[5,8,128]{2,1,0:T(8,128)S(1)} collective-permute-done((f32[5,8,128]{2,1,0:T(8,128)S(1)}, f32[5,8,128]{2,1,0:T(8,128)S(1)}, u32[]{:S(2)}, u32[]{:S(2)}) %collective-permute-start.5) | collective-permute-done | bytes 20512 | tf_op jit(solution)/shard_map/ppermute | solution.py:235
  25.0 0.0 collective-permute-done.6.refs_3_
  25.0 1.1 %render.1 = f32[2,2,16]{2,1,0:T(2,128)} custom-call(f32[5,8,128]{2,1,0:T(8,128)S(1)} %get-tuple-element.23.refs_0_, f32[5,8,128]{2,1,0:T(8,128)S(1)} %collective-permute-done.4.refs_1_, f32[5,8,128]{2,1,0:T(8,128)S(1)} %collective-permute-done.5.refs_2_, f32[5,8,128]{2,1,0:T(8,128)S(1)} %collective-permute-done.6.refs_3_), custom_call_target="tpu_custom_call" | custom-call | tf_op jit(solution)/shard_map/render/pallas_call | solution.py:236
Async XLA Ops:
  0.0 13.0 %copy-start = (s32[64,32]{0,1:T(8,128)S(1)}, s32[64,32]{0,1:T(8,128)}, u32[]{:S(2)}) copy-start(s32[64,32]{0,1:T(8,128)} %param.5) | copy-start | bytes 24580
  1.4 9.4 %collective-permute-start = (f32[65,8,128]{2,1,0:T(8,128)S(1)}, f32[65,8,128]{2,1,0:T(8,128)S(1)}, u32[]{:S(2)}, u32[]{:S(2)}) collective-permute-start(f32[65,8,128]{2,1,0:T(8,128)S(1)} %get-tuple-element.17), channel_id=1, source_target_pairs={{0,16},{16,32},{32,48},{48,64},{64,80},{80,96},{96,112},{112,128},... | collective-permute-start | bytes 798728 | tf_op jit(solution)/shard_map/ppermute | solution.py:207
  1.4 11.6 %collective-permute-start.1 = (f32[65,8,128]{2,1,0:T(8,128)S(1)}, f32[65,8,128]{2,1,0:T(8,128)S(1)}, u32[]{:S(2)}, u32[]{:S(2)}) collective-permute-start(f32[65,8,128]{2,1,0:T(8,128)S(1)} %get-tuple-element.18), channel_id=1, source_target_pairs={{0,224},{16,240},{32,0},{48,16},{64,32},{80,48},{96,64},{112,80},{... | collective-permute-start | bytes 798728 | tf_op jit(solution)/shard_map/ppermute | solution.py:207
  7.3 9.2 %collective-permute-start.2 = (f32[65,8,128]{2,1,0:T(8,128)S(1)}, f32[65,8,128]{2,1,0:T(8,128)S(1)}, u32[]{:S(2)}, u32[]{:S(2)}) collective-permute-start(f32[65,8,128]{2,1,0:T(8,128)S(1)} %get-tuple-element.21), channel_id=1, source_target_pairs={{0,32},{16,48},{32,64},{48,80},{64,96},{80,112},{96,128},{112,144}... | collective-permute-start | bytes 798728 | tf_op jit(solution)/shard_map/ppermute | solution.py:207
  7.3 9.2 %collective-permute-start.3 = (f32[65,8,128]{2,1,0:T(8,128)S(1)}, f32[65,8,128]{2,1,0:T(8,128)S(1)}, u32[]{:S(2)}, u32[]{:S(2)}) collective-permute-start(f32[65,8,128]{2,1,0:T(8,128)S(1)} %get-tuple-element.22), channel_id=1, source_target_pairs={{0,240},{16,0},{32,16},{48,32},{64,48},{80,64},{96,80},{112,96},{1... | collective-permute-start | bytes 798728 | tf_op jit(solution)/shard_map/ppermute | solution.py:207
  16.9 5.4 %collective-permute-start.4 = (f32[5,8,128]{2,1,0:T(8,128)S(1)}, f32[5,8,128]{2,1,0:T(8,128)S(1)}, u32[]{:S(2)}, u32[]{:S(2)}) collective-permute-start(f32[5,8,128]{2,1,0:T(8,128)S(1)} %get-tuple-element.24), channel_id=1, source_target_pairs={{0,3},{1,2},{2,0},{3,1},{4,7},{5,6},{6,4},{7,5},{8,11},{9,10},{10,... | collective-permute-start | bytes 61448 | tf_op jit(solution)/shard_map/ppermute | solution.py:235
  20.0 5.0 %collective-permute-start.5 = (f32[5,8,128]{2,1,0:T(8,128)S(1)}, f32[5,8,128]{2,1,0:T(8,128)S(1)}, u32[]{:S(2)}, u32[]{:S(2)}) collective-permute-start(f32[5,8,128]{2,1,0:T(8,128)S(1)} %get-tuple-element.25), channel_id=1, source_target_pairs={{0,2},{1,3},{2,1},{3,0},{4,6},{5,7},{6,5},{7,4},{8,10},{9,11},{10,... | collective-permute-start | bytes 61448 | tf_op jit(solution)/shard_map/ppermute | solution.py:235
  20.5 4.5 %collective-permute-start.6 = (f32[5,8,128]{2,1,0:T(8,128)S(1)}, f32[5,8,128]{2,1,0:T(8,128)S(1)}, u32[]{:S(2)}, u32[]{:S(2)}) collective-permute-start(f32[5,8,128]{2,1,0:T(8,128)S(1)} %get-tuple-element.26), channel_id=1, source_target_pairs={{0,1},{1,0},{2,3},{3,2},{4,5},{5,4},{6,7},{7,6},{8,9},{9,8},{10,11... | collective-permute-start | bytes 61448 | tf_op jit(solution)/shard_map/ppermute | solution.py:235

commit v5 on v4

--- a/solution.py
+++ b/solution.py
@@ -20,9 +20,9 @@
 NONE = BRICKS
 VMEM_BYTES = 4 << 20
 
-MOVES = (1, 2, -2, -1)
-EARLY = (0, 2)
-LATE = (1, 3)
+MOVES = ((1, 1), (2, -2), (-2, 2), (-1, -1))
+EARLY = (0, 1)
+LATE = (2, 3)
 PLACES = len(MOVES) + 1
 SENDS = ((3, 2, 0, 1), (2, 3, 1, 0), (1, 0, 3, 2))
 TILES = BRICKS // 2
@@ -59,8 +59,10 @@
     row = lax.broadcasted_iota(jnp.int32, (8, 128), 0)
     home_copy.wait()
     chosen = []
-    for move, out_ref in zip(MOVES + (0,), outs):
-        bricks = find_bricks(home_ref, lax.rem(position + (move + GROUP), GROUP))
+    odd = (position & 1) == 1
+    for (step, odd_step), out_ref in zip(MOVES + ((0, 0),), outs):
+        target = (position + jnp.where(odd, odd_step, step) + GROUP) & (GROUP - 1)
+        bricks = find_bricks(home_ref, target)
         labels = [slot_label(home_ref, brick) for brick in bricks]
         out_ref[CAP * ROWS] = jnp.where(row == 0, labels[0], labels[1]).astype(jnp.float32)
         chosen.append([jnp.minimum(brick, BRICKS - 1) for brick in bricks])
@@ -203,7 +205,7 @@
     )(home, density)
     arrived = []
     for move, bricks in zip(MOVES, packed):
-        pairs = [(source, (source + move) % GROUP) for source in range(GROUP)]
+        pairs = [(source, (source + move[source % 2]) % GROUP) for source in range(GROUP)]
         arrived.append(lax.ppermute(bricks, "gx", pairs))
     sample_box = (BRICKS + 1, QUARTERS, 8, 128)
     peak_box = (QUARTERS, 2 * BRICKS, 128)

time: 26.2 us -> 25.5 us (0.973)
  waiting for transfers between devices: 8.95 us -> 8.3 us
    ppermute x4, waiting for transfers between devices: 6.05 us -> 5.4 us  [shards(): arrived.append(lax.ppermute(bricks, 'gx', pairs))]
where the time goes in v5:
time: 25.5 us; the launch traced here: 25.4 us
  starting transfers between devices  13.3 us (52%)
  waiting for transfers between devices  8.3 us (33%)
  Pallas kernels  3.82 us (15%)
    ppermute x4, starting transfers between devices, shards(): arrived.append(lax.ppermute(bricks, 'gx', pairs))  8.07 us
    ppermute x4, waiting for transfers between devices, shards(): arrived.append(lax.ppermute(bricks, 'gx', pairs))  5.4 us
    ppermute x3, starting transfers between devices, shards(): others.append(lax.ppermute(message, 'gz', list(enumerate(table))))  5.18 us
    ppermute x3, waiting for transfers between devices, shards(): others.append(lax.ppermute(message, 'gz', list(enumerate(table))))  2.9 us
    pallas_call x1, Pallas kernels, shards(): pl.pallas_call(pack_kernel, out_shape=[box] * PLACES, in_specs=[hbm, hbm]...  1.34 us
    pallas_call x1, Pallas kernels, shards(): pl.pallas_call(render_kernel, out_shape=jax.ShapeDtypeStruct((2, 8 // PIX...  1.1 us
    pallas_call x1, Pallas kernels, shards(): pl.pallas_call(early_kernel, out_shape=[jax.ShapeDtypeStruct(sample_box,...  0.98 us
  transfers between devices with their start and end apart: 7, of which 5 were waited for; matrix products, arithmetic and copies ran while one was open for 0% of the time, Pallas kernels for 4%

profile of v5, /device:TPU:2, one launch (start us, length us, event | category | flops | bytes accessed | tf_op | source)
XLA Modules:
  0.0 25.4 jit_solution(14584738801631180861)
XLA Ops:
  0.0 0.0 copy-start
  0.0 1.3 %pack.1 = (f32[65,8,128]{2,1,0:T(8,128)S(1)}, f32[65,8,128]{2,1,0:T(8,128)S(1)}, f32[65,8,128]{2,1,0:T(8,128)S(1)}, f32[65,8,128]{2,1,0:T(8,128)S(1)}, f32[65,8,128]{2,1,0:T(8,128)S(1)}) custom-call(s32[8]{0:T(128)} %bitcast.7, f32[8,32,8,128]{3,2,1,0:T(8,128)} %bitcast.6), custom_call_target="tpu_custom_call" | custom-call | tf_op jit(solution)/shard_map/pack/pallas_call | solution.py:192
  1.4 0.0 collective-permute-start
  1.4 2.0 %collective-permute-start.1 = (f32[65,8,128]{2,1,0:T(8,128)S(1)}, f32[65,8,128]{2,1,0:T(8,128)S(1)}, u32[]{:S(2)}, u32[]{:S(2)}) collective-permute-start(f32[65,8,128]{2,1,0:T(8,128)S(1)} %get-tuple-element.18), channel_id=1, source_target_pairs={{0,32},{16,240},{32,64},{48,16},{64,96},{80,48},{96,128},{112,80},... | collective-permute-start | bytes 798728 | tf_op jit(solution)/shard_map/ppermute | solution.py:209
  3.4 4.0 %collective-permute-start.2 = (f32[65,8,128]{2,1,0:T(8,128)S(1)}, f32[65,8,128]{2,1,0:T(8,128)S(1)}, u32[]{:S(2)}, u32[]{:S(2)}) collective-permute-start(f32[65,8,128]{2,1,0:T(8,128)S(1)} %get-tuple-element.21), channel_id=1, source_target_pairs={{0,224},{16,48},{32,0},{48,80},{64,32},{80,112},{96,64},{112,144},... | collective-permute-start | bytes 798728 | tf_op jit(solution)/shard_map/ppermute | solution.py:209
  7.4 2.0 %collective-permute-start.3 = (f32[65,8,128]{2,1,0:T(8,128)S(1)}, f32[65,8,128]{2,1,0:T(8,128)S(1)}, u32[]{:S(2)}, u32[]{:S(2)}) collective-permute-start(f32[65,8,128]{2,1,0:T(8,128)S(1)} %get-tuple-element.22), channel_id=1, source_target_pairs={{0,240},{16,0},{32,16},{48,32},{64,48},{80,64},{96,80},{112,96},{1... | collective-permute-start | bytes 798728 | tf_op jit(solution)/shard_map/ppermute | solution.py:209
  9.4 3.2 %collective-permute-done.refs_1_ = f32[65,8,128]{2,1,0:T(8,128)S(1)} collective-permute-done((f32[65,8,128]{2,1,0:T(8,128)S(1)}, f32[65,8,128]{2,1,0:T(8,128)S(1)}, u32[]{:S(2)}, u32[]{:S(2)}) %collective-permute-start) | collective-permute-done | bytes 266272 | tf_op jit(solution)/shard_map/ppermute | solution.py:209
  12.7 1.9 %collective-permute-done.1.refs_2_ = f32[65,8,128]{2,1,0:T(8,128)S(1)} collective-permute-done((f32[65,8,128]{2,1,0:T(8,128)S(1)}, f32[65,8,128]{2,1,0:T(8,128)S(1)}, u32[]{:S(2)}, u32[]{:S(2)}) %collective-permute-start.1) | collective-permute-done | bytes 266272 | tf_op jit(solution)/shard_map/ppermute | solution.py:209
  14.5 0.0 copy-done
  14.5 1.0 %early.1 = (f32[9,4,8,128]{3,2,1,0:T(8,128)S(1)}, f32[4,16,128]{2,1,0:T(8,128)S(1)}) custom-call(s32[32,64]{1,0:T(8,128)S(1)} %bitcast.4, f32[65,8,128]{2,1,0:T(8,128)S(1)} %get-tuple-element.16.refs_0_, f32[65,8,128]{2,1,0:T(8,128)S(1)} %collective-permute-done.refs_1_, f32[65,8,128]{2,1,0:T(8,128)S(1)} %collective-permute-done.1.refs_2_), custom_call_target="tpu_custom_call" | custom-call | tf_op jit(solution)/shard_map/early/pallas_call | solution.py:212
  15.5 0.0 collective-permute-done.2.refs_0_
  15.5 0.3 %collective-permute-done.3.refs_1_ = f32[65,8,128]{2,1,0:T(8,128)S(1)} collective-permute-done((f32[65,8,128]{2,1,0:T(8,128)S(1)}, f32[65,8,128]{2,1,0:T(8,128)S(1)}, u32[]{:S(2)}, u32[]{:S(2)}) %collective-permute-start.3) | collective-permute-done | bytes 266272 | tf_op jit(solution)/shard_map/ppermute | solution.py:209
  15.8 0.4 %late.1 = (f32[5,8,128]{2,1,0:T(8,128)S(1)}, f32[5,8,128]{2,1,0:T(8,128)S(1)}, f32[5,8,128]{2,1,0:T(8,128)S(1)}, f32[5,8,128]{2,1,0:T(8,128)S(1)}) custom-call(s32[32,64]{1,0:T(8,128)S(1)} %bitcast.5, f32[9,4,8,128]{3,2,1,0:T(8,128)S(1)} %get-tuple-element.19.early_samples, f32[4,16,128]{2,1,0:T(8,128)S(1)} %get-tuple-element.20.early_peaks, ...), custom_call_target="tpu_custom_call" | custom-call | tf_op jit(solution)/shard_map/late/pallas_call | solution.py:223
  16.2 3.1 %collective-permute-start.4 = (f32[5,8,128]{2,1,0:T(8,128)S(1)}, f32[5,8,128]{2,1,0:T(8,128)S(1)}, u32[]{:S(2)}, u32[]{:S(2)}) collective-permute-start(f32[5,8,128]{2,1,0:T(8,128)S(1)} %get-tuple-element.24), channel_id=1, source_target_pairs={{0,3},{1,2},{2,0},{3,1},{4,7},{5,6},{6,4},{7,5},{8,11},{9,10},{10,... | collective-permute-start | bytes 61448 | tf_op jit(solution)/shard_map/ppermute | solution.py:237
  19.3 0.5 %collective-permute-start.5 = (f32[5,8,128]{2,1,0:T(8,128)S(1)}, f32[5,8,128]{2,1,0:T(8,128)S(1)}, u32[]{:S(2)}, u32[]{:S(2)}) collective-permute-start(f32[5,8,128]{2,1,0:T(8,128)S(1)} %get-tuple-element.25), channel_id=1, source_target_pairs={{0,2},{1,3},{2,1},{3,0},{4,6},{5,7},{6,5},{7,4},{8,10},{9,11},{10,... | collective-permute-start | bytes 61448 | tf_op jit(solution)/shard_map/ppermute | solution.py:237
  19.8 1.6 %collective-permute-start.6 = (f32[5,8,128]{2,1,0:T(8,128)S(1)}, f32[5,8,128]{2,1,0:T(8,128)S(1)}, u32[]{:S(2)}, u32[]{:S(2)}) collective-permute-start(f32[5,8,128]{2,1,0:T(8,128)S(1)} %get-tuple-element.26), channel_id=1, source_target_pairs={{0,1},{1,0},{2,3},{3,2},{4,5},{5,4},{6,7},{7,6},{8,9},{9,8},{10,11... | collective-permute-start | bytes 61448 | tf_op jit(solution)/shard_map/ppermute | solution.py:237
  21.4 0.2 collective-permute-done.4.refs_1_
  21.6 2.7 %collective-permute-done.5.refs_2_ = f32[5,8,128]{2,1,0:T(8,128)S(1)} collective-permute-done((f32[5,8,128]{2,1,0:T(8,128)S(1)}, f32[5,8,128]{2,1,0:T(8,128)S(1)}, u32[]{:S(2)}, u32[]{:S(2)}) %collective-permute-start.5) | collective-permute-done | bytes 20512 | tf_op jit(solution)/shard_map/ppermute | solution.py:237
  24.3 0.0 collective-permute-done.6.refs_3_
  24.3 1.1 %render.1 = f32[2,2,16]{2,1,0:T(2,128)} custom-call(f32[5,8,128]{2,1,0:T(8,128)S(1)} %get-tuple-element.23.refs_0_, f32[5,8,128]{2,1,0:T(8,128)S(1)} %collective-permute-done.4.refs_1_, f32[5,8,128]{2,1,0:T(8,128)S(1)} %collective-permute-done.5.refs_2_, f32[5,8,128]{2,1,0:T(8,128)S(1)} %collective-permute-done.6.refs_3_), custom_call_target="tpu_custom_call" | custom-call | tf_op jit(solution)/shard_map/render/pallas_call | solution.py:238
Async XLA Ops:
  0.0 14.5 %copy-start = (s32[64,32]{0,1:T(8,128)S(1)}, s32[64,32]{0,1:T(8,128)}, u32[]{:S(2)}) copy-start(s32[64,32]{0,1:T(8,128)} %param.5) | copy-start | bytes 24580
  1.4 11.3 %collective-permute-start = (f32[65,8,128]{2,1,0:T(8,128)S(1)}, f32[65,8,128]{2,1,0:T(8,128)S(1)}, u32[]{:S(2)}, u32[]{:S(2)}) collective-permute-start(f32[65,8,128]{2,1,0:T(8,128)S(1)} %get-tuple-element.17), channel_id=1, source_target_pairs={{0,16},{16,32},{32,48},{48,64},{64,80},{80,96},{96,112},{112,128},... | collective-permute-start | bytes 798728 | tf_op jit(solution)/shard_map/ppermute | solution.py:209
  1.4 13.2 %collective-permute-start.1 = (f32[65,8,128]{2,1,0:T(8,128)S(1)}, f32[65,8,128]{2,1,0:T(8,128)S(1)}, u32[]{:S(2)}, u32[]{:S(2)}) collective-permute-start(f32[65,8,128]{2,1,0:T(8,128)S(1)} %get-tuple-element.18), channel_id=1, source_target_pairs={{0,32},{16,240},{32,64},{48,16},{64,96},{80,48},{96,128},{112,80},... | collective-permute-start | bytes 798728 | tf_op jit(solution)/shard_map/ppermute | solution.py:209
  3.4 12.2 %collective-permute-start.2 = (f32[65,8,128]{2,1,0:T(8,128)S(1)}, f32[65,8,128]{2,1,0:T(8,128)S(1)}, u32[]{:S(2)}, u32[]{:S(2)}) collective-permute-start(f32[65,8,128]{2,1,0:T(8,128)S(1)} %get-tuple-element.21), channel_id=1, source_target_pairs={{0,224},{16,48},{32,0},{48,80},{64,32},{80,112},{96,64},{112,144},... | collective-permute-start | bytes 798728 | tf_op jit(solution)/shard_map/ppermute | solution.py:209
  7.4 8.4 %collective-permute-start.3 = (f32[65,8,128]{2,1,0:T(8,128)S(1)}, f32[65,8,128]{2,1,0:T(8,128)S(1)}, u32[]{:S(2)}, u32[]{:S(2)}) collective-permute-start(f32[65,8,128]{2,1,0:T(8,128)S(1)} %get-tuple-element.22), channel_id=1, source_target_pairs={{0,240},{16,0},{32,16},{48,32},{64,48},{80,64},{96,80},{112,96},{1... | collective-permute-start | bytes 798728 | tf_op jit(solution)/shard_map/ppermute | solution.py:209
  16.2 5.4 %collective-permute-start.4 = (f32[5,8,128]{2,1,0:T(8,128)S(1)}, f32[5,8,128]{2,1,0:T(8,128)S(1)}, u32[]{:S(2)}, u32[]{:S(2)}) collective-permute-start(f32[5,8,128]{2,1,0:T(8,128)S(1)} %get-tuple-element.24), channel_id=1, source_target_pairs={{0,3},{1,2},{2,0},{3,1},{4,7},{5,6},{6,4},{7,5},{8,11},{9,10},{10,... | collective-permute-start | bytes 61448 | tf_op jit(solution)/shard_map/ppermute | solution.py:237
  19.3 5.0 %collective-permute-start.5 = (f32[5,8,128]{2,1,0:T(8,128)S(1)}, f32[5,8,128]{2,1,0:T(8,128)S(1)}, u32[]{:S(2)}, u32[]{:S(2)}) collective-permute-start(f32[5,8,128]{2,1,0:T(8,128)S(1)} %get-tuple-element.25), channel_id=1, source_target_pairs={{0,2},{1,3},{2,1},{3,0},{4,6},{5,7},{6,5},{7,4},{8,10},{9,11},{10,... | collective-permute-start | bytes 61448 | tf_op jit(solution)/shard_map/ppermute | solution.py:237
  19.8 4.5 %collective-permute-start.6 = (f32[5,8,128]{2,1,0:T(8,128)S(1)}, f32[5,8,128]{2,1,0:T(8,128)S(1)}, u32[]{:S(2)}, u32[]{:S(2)}) collective-permute-start(f32[5,8,128]{2,1,0:T(8,128)S(1)} %get-tuple-element.26), channel_id=1, source_target_pairs={{0,1},{1,0},{2,3},{3,2},{4,5},{5,4},{6,7},{7,6},{8,9},{9,8},{10,11... | collective-permute-start | bytes 61448 | tf_op jit(solution)/shard_map/ppermute | solution.py:237

commit v6 on v5

--- a/solution.py
+++ b/solution.py
@@ -103,9 +103,13 @@
             peak_ref[quarter, pl.ds(slot, 1), :] = jnp.max(peak, axis=0, keepdims=True)
 
 
-def early_kernel(jitter_ref, *refs):
-    arrived = refs[: len(EARLY) + 1]
-    sample_ref, peak_ref = refs[len(EARLY) + 1 :]
+def stay_kernel(jitter_ref, stayed, sample_ref, peak_ref):
+    take_samples(jitter_ref, [stayed], sample_ref, peak_ref)
+
+
+def early_kernel(jitter_ref, stay_samples, stay_peaks, *refs):
+    del stay_samples, stay_peaks
+    arrived, (sample_ref, peak_ref) = refs[: len(EARLY)], refs[len(EARLY) :]
     take_samples(jitter_ref, arrived, sample_ref, peak_ref)
 
 
@@ -145,17 +149,21 @@
     absorb = jnp.float32(DEPTH_GAIN / (8 * LAYERS))
     light = jnp.zeros((8, 128), jnp.float32)
     cover = jnp.zeros((8, 128), jnp.float32)
-    picked = (lane & 3) * 32
+    picked = [(lane & 3) * 32 + x * 8 for x in range(PIXEL)]
     for tile in range(tiles):
         majorant = jnp.where(lane < 64, peak[2 * tile : 2 * tile + 1], peak[2 * tile + 1 : 2 * tile + 2])
+        scale = absorb / majorant
         through = None
         radiance = None
         for depth in range(LAYERS):
             samples = held_ref[depth, tile]
-            ratio = absorb * samples / majorant
+            after = pltpu.roll(samples, 127, 1)
+            ratio = samples * scale
+            next_ratio = after * scale
             passed = 1.0 - ratio
-            shone = ratio * (GLOW * samples)
-            for span in (1, 2, 4):
+            shone = ratio * (GLOW * samples) + passed * (next_ratio * (GLOW * after))
+            passed = passed * (1.0 - next_ratio)
+            for span in (2, 4):
                 shone = shone + passed * pltpu.roll(shone, 128 - span, 1)
                 passed = passed * pltpu.roll(passed, 128 - span, 1)
             if depth == 0:
@@ -163,21 +171,21 @@
             else:
                 radiance = radiance + through * shone
                 through = through * passed
-        opacity = 1.0 - through
         pooled = []
-        for field in (radiance, opacity):
-            field = field + pltpu.roll(field, 120, 1)
-            field = field + pltpu.roll(field, 112, 1)
-            field = field + pltpu.roll(field, 7, 0)
-            field = field + pltpu.roll(field, 6, 0)
-            pooled.append(jnp.take_along_axis(field, picked, axis=1, mode="promise_in_bounds"))
+        for field in (radiance, 1.0 - through):
+            parts = [
+                jnp.take_along_axis(field, where_at, axis=1, mode="promise_in_bounds")
+                for where_at in picked
+            ]
+            pooled.append((parts[0] + parts[1]) + (parts[2] + parts[3]))
         here = (lane >> 2) == tile
         light = jnp.where(here, pooled[0], light)
         cover = jnp.where(here, pooled[1], cover)
-    scale = jnp.float32(1.0 / (PIXEL * PIXEL))
+    mean = jnp.float32(1.0 / (PIXEL * PIXEL))
     for number, field in enumerate((light, cover)):
         for pixel in range(8 // PIXEL):
-            out_ref[number, pixel : pixel + 1, :] = field[pixel * PIXEL : pixel * PIXEL + 1, :16] * scale
+            rows = field[pixel * PIXEL : (pixel + 1) * PIXEL, :16]
+            out_ref[number, pixel : pixel + 1, :] = jnp.sum(rows, axis=0, keepdims=True) * mean
 
 
 def shards(sim_density, brick_home, jitter):
@@ -209,17 +217,27 @@
         arrived.append(lax.ppermute(bricks, "gx", pairs))
     sample_box = (BRICKS + 1, QUARTERS, 8, 128)
     peak_box = (QUARTERS, 2 * BRICKS, 128)
+    boxes = [
+        jax.ShapeDtypeStruct(sample_box, jnp.float32),
+        jax.ShapeDtypeStruct(peak_box, jnp.float32),
+    ]
+    stayed = pl.pallas_call(
+        stay_kernel,
+        out_shape=boxes,
+        in_specs=[vmem] * 2,
+        out_specs=[vmem] * 2,
+        compiler_params=params,
+        name="stay",
+    )(jitter.T, packed[-1])
     gathered = pl.pallas_call(
         early_kernel,
-        out_shape=[
-            jax.ShapeDtypeStruct(sample_box, jnp.float32),
-            jax.ShapeDtypeStruct(peak_box, jnp.float32),
-        ],
-        in_specs=[vmem] * (2 + len(EARLY)),
+        out_shape=boxes,
+        in_specs=[vmem] * (3 + len(EARLY)),
         out_specs=[vmem] * 2,
+        input_output_aliases={1: 0, 2: 1},
         compiler_params=params,
         name="early",
-    )(jitter.T, packed[-1], *[arrived[number] for number in EARLY])
+    )(jitter.T, *stayed, *[arrived[number] for number in EARLY])
     messages = pl.pallas_call(
         late_kernel,
         out_shape=[jax.ShapeDtypeStruct((TILES + 1, 8, 128), jnp.float32)] * LAYERS,

time: 25.5 us -> 25.4 us (level)
  Pallas kernels: 3.82 us -> 3.42 us
  waiting for transfers between devices: 8.3 us -> 8.58 us
    pallas_call x1 -> x2, Pallas kernels: 0.98 us -> 0.69 us  [the longest x1 0.39 us: shards(): pl.pallas_call(early_kernel, out_shape=boxes, in_specs=[vmem] * (3 + len(...]
    ppermute x4, waiting for transfers between devices: 5.4 us -> 5.68 us  [shards(): arrived.append(lax.ppermute(bricks, 'gx', pairs))]
  transfers between devices with their start and end apart: 7 -> 7, of which waited for: 5 -> 5; matrix products, arithmetic and copies ran while one was open for 0% -> 0% of each run, Pallas kernels for 4% -> 3%
where the time goes in v6:
time: 25.4 us; the launch traced here: 25.3 us
  starting transfers between devices  13.3 us (52%)
  waiting for transfers between devices  8.58 us (34%)
  Pallas kernels  3.42 us (13%)
    ppermute x4, starting transfers between devices, shards(): arrived.append(lax.ppermute(bricks, 'gx', pairs))  8.07 us
    ppermute x4, waiting for transfers between devices, shards(): arrived.append(lax.ppermute(bricks, 'gx', pairs))  5.68 us
    ppermute x3, starting transfers between devices, shards(): others.append(lax.ppermute(message, 'gz', list(enumerate(table))))  5.18 us
    ppermute x3, waiting for transfers between devices, shards(): others.append(lax.ppermute(message, 'gz', list(enumerate(table))))  2.9 us
    pallas_call x1, Pallas kernels, shards(): pl.pallas_call(pack_kernel, out_shape=[box] * PLACES, in_specs=[hbm, hbm]...  1.34 us
    pallas_call x1, Pallas kernels, shards(): pl.pallas_call(render_kernel, out_shape=jax.ShapeDtypeStruct((2, 8 // PIX...  0.98 us
  transfers between devices with their start and end apart: 7, of which 5 were waited for; matrix products, arithmetic and copies ran while one was open for 0% of the time, Pallas kernels for 3%

profile of v6, /device:TPU:2, one launch (start us, length us, event | category | flops | bytes accessed | tf_op | source)
XLA Modules:
  0.0 25.3 jit_solution(11458567871780906336)
XLA Ops:
  0.0 0.0 copy-start
  0.0 1.3 %pack.1 = (f32[65,8,128]{2,1,0:T(8,128)S(1)}, f32[65,8,128]{2,1,0:T(8,128)S(1)}, f32[65,8,128]{2,1,0:T(8,128)S(1)}, f32[65,8,128]{2,1,0:T(8,128)S(1)}, f32[65,8,128]{2,1,0:T(8,128)S(1)}) custom-call(s32[8]{0:T(128)} %bitcast.8, f32[8,32,8,128]{3,2,1,0:T(8,128)} %bitcast.7), custom_call_target="tpu_custom_call" | custom-call | tf_op jit(solution)/shard_map/pack/pallas_call | solution.py:200
  1.4 0.0 collective-permute-start
  1.4 2.0 %collective-permute-start.1 = (f32[65,8,128]{2,1,0:T(8,128)S(1)}, f32[65,8,128]{2,1,0:T(8,128)S(1)}, u32[]{:S(2)}, u32[]{:S(2)}) collective-permute-start(f32[65,8,128]{2,1,0:T(8,128)S(1)} %get-tuple-element.22), channel_id=1, source_target_pairs={{0,32},{16,240},{32,64},{48,16},{64,96},{80,48},{96,128},{112,80},... | collective-permute-start | bytes 798728 | tf_op jit(solution)/shard_map/ppermute | solution.py:217
  3.4 4.0 %collective-permute-start.2 = (f32[65,8,128]{2,1,0:T(8,128)S(1)}, f32[65,8,128]{2,1,0:T(8,128)S(1)}, u32[]{:S(2)}, u32[]{:S(2)}) collective-permute-start(f32[65,8,128]{2,1,0:T(8,128)S(1)} %get-tuple-element.25), channel_id=1, source_target_pairs={{0,224},{16,48},{32,0},{48,80},{64,32},{80,112},{96,64},{112,144},... | collective-permute-start | bytes 798728 | tf_op jit(solution)/shard_map/ppermute | solution.py:217
  7.4 2.0 %collective-permute-start.3 = (f32[65,8,128]{2,1,0:T(8,128)S(1)}, f32[65,8,128]{2,1,0:T(8,128)S(1)}, u32[]{:S(2)}, u32[]{:S(2)}) collective-permute-start(f32[65,8,128]{2,1,0:T(8,128)S(1)} %get-tuple-element.26), channel_id=1, source_target_pairs={{0,240},{16,0},{32,16},{48,32},{64,48},{80,64},{96,80},{112,96},{1... | collective-permute-start | bytes 798728 | tf_op jit(solution)/shard_map/ppermute | solution.py:217
  9.4 0.0 copy-done
  9.4 0.3 %stay.1 = (f32[9,4,8,128]{3,2,1,0:T(8,128)S(1)}, f32[4,16,128]{2,1,0:T(8,128)S(1)}) custom-call(s32[32,64]{1,0:T(8,128)S(1)} %bitcast.4, f32[65,8,128]{2,1,0:T(8,128)S(1)} %get-tuple-element.18.stayed), custom_call_target="tpu_custom_call" | custom-call | tf_op jit(solution)/shard_map/stay/pallas_call | solution.py:224
  9.7 2.9 %collective-permute-done.refs_0_ = f32[65,8,128]{2,1,0:T(8,128)S(1)} collective-permute-done((f32[65,8,128]{2,1,0:T(8,128)S(1)}, f32[65,8,128]{2,1,0:T(8,128)S(1)}, u32[]{:S(2)}, u32[]{:S(2)}) %collective-permute-start) | collective-permute-done | bytes 266272 | tf_op jit(solution)/shard_map/ppermute | solution.py:217
  12.7 1.9 %collective-permute-done.1.refs_1_ = f32[65,8,128]{2,1,0:T(8,128)S(1)} collective-permute-done((f32[65,8,128]{2,1,0:T(8,128)S(1)}, f32[65,8,128]{2,1,0:T(8,128)S(1)}, u32[]{:S(2)}, u32[]{:S(2)}) %collective-permute-start.1) | collective-permute-done | bytes 266272 | tf_op jit(solution)/shard_map/ppermute | solution.py:217
  14.5 0.4 %early.1 = (f32[9,4,8,128]{3,2,1,0:T(8,128)S(1)}, f32[4,16,128]{2,1,0:T(8,128)S(1)}) custom-call(s32[32,64]{1,0:T(8,128)S(1)} %bitcast.5, f32[9,4,8,128]{3,2,1,0:T(8,128)S(1)} %get-tuple-element.19.stay_samples, f32[4,16,128]{2,1,0:T(8,128)S(1)} %get-tuple-element.20.stay_peaks, ...), custom_call_target="tpu_custom_call", output_to_operand_aliasing={{0}: (1, {}), {1}: (2, {})} | custom-call | tf_op jit(solution)/shard_map/early/pallas_call | solution.py:232
  14.9 0.0 collective-permute-done.2.refs_0_
  14.9 0.9 %collective-permute-done.3.refs_1_ = f32[65,8,128]{2,1,0:T(8,128)S(1)} collective-permute-done((f32[65,8,128]{2,1,0:T(8,128)S(1)}, f32[65,8,128]{2,1,0:T(8,128)S(1)}, u32[]{:S(2)}, u32[]{:S(2)}) %collective-permute-start.3) | collective-permute-done | bytes 266272 | tf_op jit(solution)/shard_map/ppermute | solution.py:217
  15.8 0.4 %late.1 = (f32[5,8,128]{2,1,0:T(8,128)S(1)}, f32[5,8,128]{2,1,0:T(8,128)S(1)}, f32[5,8,128]{2,1,0:T(8,128)S(1)}, f32[5,8,128]{2,1,0:T(8,128)S(1)}) custom-call(s32[32,64]{1,0:T(8,128)S(1)} %bitcast.6, f32[9,4,8,128]{3,2,1,0:T(8,128)S(1)} %get-tuple-element.23.early_samples, f32[4,16,128]{2,1,0:T(8,128)S(1)} %get-tuple-element.24.early_peaks, ...), custom_call_target="tpu_custom_call" | custom-call | tf_op jit(solution)/shard_map/late/pallas_call | solution.py:241
  16.2 3.1 %collective-permute-start.4 = (f32[5,8,128]{2,1,0:T(8,128)S(1)}, f32[5,8,128]{2,1,0:T(8,128)S(1)}, u32[]{:S(2)}, u32[]{:S(2)}) collective-permute-start(f32[5,8,128]{2,1,0:T(8,128)S(1)} %get-tuple-element.28), channel_id=1, source_target_pairs={{0,3},{1,2},{2,0},{3,1},{4,7},{5,6},{6,4},{7,5},{8,11},{9,10},{10,... | collective-permute-start | bytes 61448 | tf_op jit(solution)/shard_map/ppermute | solution.py:255
  19.3 0.5 %collective-permute-start.5 = (f32[5,8,128]{2,1,0:T(8,128)S(1)}, f32[5,8,128]{2,1,0:T(8,128)S(1)}, u32[]{:S(2)}, u32[]{:S(2)}) collective-permute-start(f32[5,8,128]{2,1,0:T(8,128)S(1)} %get-tuple-element.29), channel_id=1, source_target_pairs={{0,2},{1,3},{2,1},{3,0},{4,6},{5,7},{6,5},{7,4},{8,10},{9,11},{10,... | collective-permute-start | bytes 61448 | tf_op jit(solution)/shard_map/ppermute | solution.py:255
  19.8 1.6 %collective-permute-start.6 = (f32[5,8,128]{2,1,0:T(8,128)S(1)}, f32[5,8,128]{2,1,0:T(8,128)S(1)}, u32[]{:S(2)}, u32[]{:S(2)}) collective-permute-start(f32[5,8,128]{2,1,0:T(8,128)S(1)} %get-tuple-element.30), channel_id=1, source_target_pairs={{0,1},{1,0},{2,3},{3,2},{4,5},{5,4},{6,7},{7,6},{8,9},{9,8},{10,11... | collective-permute-start | bytes 61448 | tf_op jit(solution)/shard_map/ppermute | solution.py:255
  21.4 0.2 collective-permute-done.4.refs_1_
  21.6 2.7 %collective-permute-done.5.refs_2_ = f32[5,8,128]{2,1,0:T(8,128)S(1)} collective-permute-done((f32[5,8,128]{2,1,0:T(8,128)S(1)}, f32[5,8,128]{2,1,0:T(8,128)S(1)}, u32[]{:S(2)}, u32[]{:S(2)}) %collective-permute-start.5) | collective-permute-done | bytes 20512 | tf_op jit(solution)/shard_map/ppermute | solution.py:255
  24.3 0.0 collective-permute-done.6.refs_3_
  24.3 1.0 %render.1 = f32[2,2,16]{2,1,0:T(2,128)} custom-call(f32[5,8,128]{2,1,0:T(8,128)S(1)} %get-tuple-element.27.refs_0_, f32[5,8,128]{2,1,0:T(8,128)S(1)} %collective-permute-done.4.refs_1_, f32[5,8,128]{2,1,0:T(8,128)S(1)} %collective-permute-done.5.refs_2_, f32[5,8,128]{2,1,0:T(8,128)S(1)} %collective-permute-done.6.refs_3_), custom_call_target="tpu_custom_call" | custom-call | tf_op jit(solution)/shard_map/render/pallas_call | solution.py:256
Async XLA Ops:
  0.0 9.4 %copy-start = (s32[64,32]{0,1:T(8,128)S(1)}, s32[64,32]{0,1:T(8,128)}, u32[]{:S(2)}) copy-start(s32[64,32]{0,1:T(8,128)} %param.5) | copy-start | bytes 24580
  1.4 11.3 %collective-permute-start = (f32[65,8,128]{2,1,0:T(8,128)S(1)}, f32[65,8,128]{2,1,0:T(8,128)S(1)}, u32[]{:S(2)}, u32[]{:S(2)}) collective-permute-start(f32[65,8,128]{2,1,0:T(8,128)S(1)} %get-tuple-element.21), channel_id=1, source_target_pairs={{0,16},{16,32},{32,48},{48,64},{64,80},{80,96},{96,112},{112,128},... | collective-permute-start | bytes 798728 | tf_op jit(solution)/shard_map/ppermute | solution.py:217
  1.4 13.2 %collective-permute-start.1 = (f32[65,8,128]{2,1,0:T(8,128)S(1)}, f32[65,8,128]{2,1,0:T(8,128)S(1)}, u32[]{:S(2)}, u32[]{:S(2)}) collective-permute-start(f32[65,8,128]{2,1,0:T(8,128)S(1)} %get-tuple-element.22), channel_id=1, source_target_pairs={{0,32},{16,240},{32,64},{48,16},{64,96},{80,48},{96,128},{112,80},... | collective-permute-start | bytes 798728 | tf_op jit(solution)/shard_map/ppermute | solution.py:217
  3.4 11.6 %collective-permute-start.2 = (f32[65,8,128]{2,1,0:T(8,128)S(1)}, f32[65,8,128]{2,1,0:T(8,128)S(1)}, u32[]{:S(2)}, u32[]{:S(2)}) collective-permute-start(f32[65,8,128]{2,1,0:T(8,128)S(1)} %get-tuple-element.25), channel_id=1, source_target_pairs={{0,224},{16,48},{32,0},{48,80},{64,32},{80,112},{96,64},{112,144},... | collective-permute-start | bytes 798728 | tf_op jit(solution)/shard_map/ppermute | solution.py:217
  7.4 8.4 %collective-permute-start.3 = (f32[65,8,128]{2,1,0:T(8,128)S(1)}, f32[65,8,128]{2,1,0:T(8,128)S(1)}, u32[]{:S(2)}, u32[]{:S(2)}) collective-permute-start(f32[65,8,128]{2,1,0:T(8,128)S(1)} %get-tuple-element.26), channel_id=1, source_target_pairs={{0,240},{16,0},{32,16},{48,32},{64,48},{80,64},{96,80},{112,96},{1... | collective-permute-start | bytes 798728 | tf_op jit(solution)/shard_map/ppermute | solution.py:217
  16.2 5.4 %collective-permute-start.4 = (f32[5,8,128]{2,1,0:T(8,128)S(1)}, f32[5,8,128]{2,1,0:T(8,128)S(1)}, u32[]{:S(2)}, u32[]{:S(2)}) collective-permute-start(f32[5,8,128]{2,1,0:T(8,128)S(1)} %get-tuple-element.28), channel_id=1, source_target_pairs={{0,3},{1,2},{2,0},{3,1},{4,7},{5,6},{6,4},{7,5},{8,11},{9,10},{10,... | collective-permute-start | bytes 61448 | tf_op jit(solution)/shard_map/ppermute | solution.py:255
  19.3 5.0 %collective-permute-start.5 = (f32[5,8,128]{2,1,0:T(8,128)S(1)}, f32[5,8,128]{2,1,0:T(8,128)S(1)}, u32[]{:S(2)}, u32[]{:S(2)}) collective-permute-start(f32[5,8,128]{2,1,0:T(8,128)S(1)} %get-tuple-element.29), channel_id=1, source_target_pairs={{0,2},{1,3},{2,1},{3,0},{4,6},{5,7},{6,5},{7,4},{8,10},{9,11},{10,... | collective-permute-start | bytes 61448 | tf_op jit(solution)/shard_map/ppermute | solution.py:255
  19.8 4.5 %collective-permute-start.6 = (f32[5,8,128]{2,1,0:T(8,128)S(1)}, f32[5,8,128]{2,1,0:T(8,128)S(1)}, u32[]{:S(2)}, u32[]{:S(2)}) collective-permute-start(f32[5,8,128]{2,1,0:T(8,128)S(1)} %get-tuple-element.30), channel_id=1, source_target_pairs={{0,1},{1,0},{2,3},{3,2},{4,5},{5,4},{6,7},{7,6},{8,9},{9,8},{10,11... | collective-permute-start | bytes 61448 | tf_op jit(solution)/shard_map/ppermute | solution.py:255

commit v7 on v6

--- a/solution.py
+++ b/solution.py
@@ -20,7 +20,7 @@
 NONE = BRICKS
 VMEM_BYTES = 4 << 20
 
-MOVES = ((1, 1), (2, -2), (-2, 2), (-1, -1))
+MOVES = ((1, 1), (-2, -2), (2, 2), (-1, -1))
 EARLY = (0, 1)
 LATE = (2, 3)
 PLACES = len(MOVES) + 1

time: 25.4 us -> 26 us (1.024)
  waiting for transfers between devices: 8.58 us -> 9.24 us
    ppermute x4, waiting for transfers between devices: 5.68 us -> 6.34 us  [shards(): arrived.append(lax.ppermute(bricks, 'gx', pairs))]
where the time goes in v7:
time: 26 us
  starting transfers between devices  13.3 us (51%)
  waiting for transfers between devices  9.24 us (36%)
  Pallas kernels  3.42 us (13%)
    ppermute x4, starting transfers between devices, shards(): arrived.append(lax.ppermute(bricks, 'gx', pairs))  8.07 us
    ppermute x4, waiting for transfers between devices, shards(): arrived.append(lax.ppermute(bricks, 'gx', pairs))  6.34 us
    ppermute x3, starting transfers between devices, shards(): others.append(lax.ppermute(message, 'gz', list(enumerate(table))))  5.18 us
    ppermute x3, waiting for transfers between devices, shards(): others.append(lax.ppermute(message, 'gz', list(enumerate(table))))  2.9 us
    pallas_call x1, Pallas kernels, shards(): pl.pallas_call(pack_kernel, out_shape=[box] * PLACES, in_specs=[hbm, hbm]...  1.34 us
    pallas_call x1, Pallas kernels, shards(): pl.pallas_call(render_kernel, out_shape=jax.ShapeDtypeStruct((2, 8 // PIX...  0.98 us
  transfers between devices with their start and end apart: 7, of which 5 were waited for; matrix products, arithmetic and copies ran while one was open for 0% of the time, Pallas kernels for 3%

profile of v7, /device:TPU:2, one launch (start us, length us, event | category | flops | bytes accessed | tf_op | source)
XLA Modules:
  0.0 26.0 jit_solution(5888499927324652422)
XLA Ops:
  0.0 0.0 copy-start
  0.0 1.3 %pack.1 = (f32[65,8,128]{2,1,0:T(8,128)S(1)}, f32[65,8,128]{2,1,0:T(8,128)S(1)}, f32[65,8,128]{2,1,0:T(8,128)S(1)}, f32[65,8,128]{2,1,0:T(8,128)S(1)}, f32[65,8,128]{2,1,0:T(8,128)S(1)}) custom-call(s32[8]{0:T(128)} %bitcast.8, f32[8,32,8,128]{3,2,1,0:T(8,128)} %bitcast.7), custom_call_target="tpu_custom_call" | custom-call | tf_op jit(solution)/shard_map/pack/pallas_call | solution.py:200
  1.4 0.0 collective-permute-start
  1.4 5.9 %collective-permute-start.1 = (f32[65,8,128]{2,1,0:T(8,128)S(1)}, f32[65,8,128]{2,1,0:T(8,128)S(1)}, u32[]{:S(2)}, u32[]{:S(2)}) collective-permute-start(f32[65,8,128]{2,1,0:T(8,128)S(1)} %get-tuple-element.22), channel_id=1, source_target_pairs={{0,224},{16,240},{32,0},{48,16},{64,32},{80,48},{96,64},{112,80},{... | collective-permute-start | bytes 798728 | tf_op jit(solution)/shard_map/ppermute | solution.py:217
  7.3 0.0 collective-permute-start.2
  7.3 2.1 %collective-permute-start.3 = (f32[65,8,128]{2,1,0:T(8,128)S(1)}, f32[65,8,128]{2,1,0:T(8,128)S(1)}, u32[]{:S(2)}, u32[]{:S(2)}) collective-permute-start(f32[65,8,128]{2,1,0:T(8,128)S(1)} %get-tuple-element.26), channel_id=1, source_target_pairs={{0,240},{16,0},{32,16},{48,32},{64,48},{80,64},{96,80},{112,96},{1... | collective-permute-start | bytes 798728 | tf_op jit(solution)/shard_map/ppermute | solution.py:217
  9.4 0.0 copy-done
  9.4 0.3 %stay.1 = (f32[9,4,8,128]{3,2,1,0:T(8,128)S(1)}, f32[4,16,128]{2,1,0:T(8,128)S(1)}) custom-call(s32[32,64]{1,0:T(8,128)S(1)} %bitcast.4, f32[65,8,128]{2,1,0:T(8,128)S(1)} %get-tuple-element.18.stayed), custom_call_target="tpu_custom_call" | custom-call | tf_op jit(solution)/shard_map/stay/pallas_call | solution.py:224
  9.7 1.0 %collective-permute-done.refs_0_ = f32[65,8,128]{2,1,0:T(8,128)S(1)} collective-permute-done((f32[65,8,128]{2,1,0:T(8,128)S(1)}, f32[65,8,128]{2,1,0:T(8,128)S(1)}, u32[]{:S(2)}, u32[]{:S(2)}) %collective-permute-start) | collective-permute-done | bytes 266272 | tf_op jit(solution)/shard_map/ppermute | solution.py:217
  10.8 2.2 %collective-permute-done.1.refs_1_ = f32[65,8,128]{2,1,0:T(8,128)S(1)} collective-permute-done((f32[65,8,128]{2,1,0:T(8,128)S(1)}, f32[65,8,128]{2,1,0:T(8,128)S(1)}, u32[]{:S(2)}, u32[]{:S(2)}) %collective-permute-start.1) | collective-permute-done | bytes 266272 | tf_op jit(solution)/shard_map/ppermute | solution.py:217
  13.0 0.4 %early.1 = (f32[9,4,8,128]{3,2,1,0:T(8,128)S(1)}, f32[4,16,128]{2,1,0:T(8,128)S(1)}) custom-call(s32[32,64]{1,0:T(8,128)S(1)} %bitcast.5, f32[9,4,8,128]{3,2,1,0:T(8,128)S(1)} %get-tuple-element.19.stay_samples, f32[4,16,128]{2,1,0:T(8,128)S(1)} %get-tuple-element.20.stay_peaks, ...), custom_call_target="tpu_custom_call", output_to_operand_aliasing={{0}: (1, {}), {1}: (2, {})} | custom-call | tf_op jit(solution)/shard_map/early/pallas_call | solution.py:232
  13.4 3.1 %collective-permute-done.2.refs_0_ = f32[65,8,128]{2,1,0:T(8,128)S(1)} collective-permute-done((f32[65,8,128]{2,1,0:T(8,128)S(1)}, f32[65,8,128]{2,1,0:T(8,128)S(1)}, u32[]{:S(2)}, u32[]{:S(2)}) %collective-permute-start.2) | collective-permute-done | bytes 266272 | tf_op jit(solution)/shard_map/ppermute | solution.py:217
  16.5 0.0 collective-permute-done.3.refs_1_
  16.5 0.4 %late.1 = (f32[5,8,128]{2,1,0:T(8,128)S(1)}, f32[5,8,128]{2,1,0:T(8,128)S(1)}, f32[5,8,128]{2,1,0:T(8,128)S(1)}, f32[5,8,128]{2,1,0:T(8,128)S(1)}) custom-call(s32[32,64]{1,0:T(8,128)S(1)} %bitcast.6, f32[9,4,8,128]{3,2,1,0:T(8,128)S(1)} %get-tuple-element.23.early_samples, f32[4,16,128]{2,1,0:T(8,128)S(1)} %get-tuple-element.24.early_peaks, ...), custom_call_target="tpu_custom_call" | custom-call | tf_op jit(solution)/shard_map/late/pallas_call | solution.py:241
  16.9 3.1 %collective-permute-start.4 = (f32[5,8,128]{2,1,0:T(8,128)S(1)}, f32[5,8,128]{2,1,0:T(8,128)S(1)}, u32[]{:S(2)}, u32[]{:S(2)}) collective-permute-start(f32[5,8,128]{2,1,0:T(8,128)S(1)} %get-tuple-element.28), channel_id=1, source_target_pairs={{0,3},{1,2},{2,0},{3,1},{4,7},{5,6},{6,4},{7,5},{8,11},{9,10},{10,... | collective-permute-start | bytes 61448 | tf_op jit(solution)/shard_map/ppermute | solution.py:255
  20.0 0.5 %collective-permute-start.5 = (f32[5,8,128]{2,1,0:T(8,128)S(1)}, f32[5,8,128]{2,1,0:T(8,128)S(1)}, u32[]{:S(2)}, u32[]{:S(2)}) collective-permute-start(f32[5,8,128]{2,1,0:T(8,128)S(1)} %get-tuple-element.29), channel_id=1, source_target_pairs={{0,2},{1,3},{2,1},{3,0},{4,6},{5,7},{6,5},{7,4},{8,10},{9,11},{10,... | collective-permute-start | bytes 61448 | tf_op jit(solution)/shard_map/ppermute | solution.py:255
  20.5 1.6 %collective-permute-start.6 = (f32[5,8,128]{2,1,0:T(8,128)S(1)}, f32[5,8,128]{2,1,0:T(8,128)S(1)}, u32[]{:S(2)}, u32[]{:S(2)}) collective-permute-start(f32[5,8,128]{2,1,0:T(8,128)S(1)} %get-tuple-element.30), channel_id=1, source_target_pairs={{0,1},{1,0},{2,3},{3,2},{4,5},{5,4},{6,7},{7,6},{8,9},{9,8},{10,11... | collective-permute-start | bytes 61448 | tf_op jit(solution)/shard_map/ppermute | solution.py:255
  22.1 0.2 collective-permute-done.4.refs_1_
  22.2 2.7 %collective-permute-done.5.refs_2_ = f32[5,8,128]{2,1,0:T(8,128)S(1)} collective-permute-done((f32[5,8,128]{2,1,0:T(8,128)S(1)}, f32[5,8,128]{2,1,0:T(8,128)S(1)}, u32[]{:S(2)}, u32[]{:S(2)}) %collective-permute-start.5) | collective-permute-done | bytes 20512 | tf_op jit(solution)/shard_map/ppermute | solution.py:255
  25.0 0.0 collective-permute-done.6.refs_3_
  25.0 1.0 %render.1 = f32[2,2,16]{2,1,0:T(2,128)} custom-call(f32[5,8,128]{2,1,0:T(8,128)S(1)} %get-tuple-element.27.refs_0_, f32[5,8,128]{2,1,0:T(8,128)S(1)} %collective-permute-done.4.refs_1_, f32[5,8,128]{2,1,0:T(8,128)S(1)} %collective-permute-done.5.refs_2_, f32[5,8,128]{2,1,0:T(8,128)S(1)} %collective-permute-done.6.refs_3_), custom_call_target="tpu_custom_call" | custom-call | tf_op jit(solution)/shard_map/render/pallas_call | solution.py:256
Async XLA Ops:
  0.0 9.4 %copy-start = (s32[64,32]{0,1:T(8,128)S(1)}, s32[64,32]{0,1:T(8,128)}, u32[]{:S(2)}) copy-start(s32[64,32]{0,1:T(8,128)} %param.5) | copy-start | bytes 24580
  1.4 9.4 %collective-permute-start = (f32[65,8,128]{2,1,0:T(8,128)S(1)}, f32[65,8,128]{2,1,0:T(8,128)S(1)}, u32[]{:S(2)}, u32[]{:S(2)}) collective-permute-start(f32[65,8,128]{2,1,0:T(8,128)S(1)} %get-tuple-element.21), channel_id=1, source_target_pairs={{0,16},{16,32},{32,48},{48,64},{64,80},{80,96},{96,112},{112,128},... | collective-permute-start | bytes 798728 | tf_op jit(solution)/shard_map/ppermute | solution.py:217
  1.4 11.6 %collective-permute-start.1 = (f32[65,8,128]{2,1,0:T(8,128)S(1)}, f32[65,8,128]{2,1,0:T(8,128)S(1)}, u32[]{:S(2)}, u32[]{:S(2)}) collective-permute-start(f32[65,8,128]{2,1,0:T(8,128)S(1)} %get-tuple-element.22), channel_id=1, source_target_pairs={{0,224},{16,240},{32,0},{48,16},{64,32},{80,48},{96,64},{112,80},{... | collective-permute-start | bytes 798728 | tf_op jit(solution)/shard_map/ppermute | solution.py:217
  7.3 9.2 %collective-permute-start.2 = (f32[65,8,128]{2,1,0:T(8,128)S(1)}, f32[65,8,128]{2,1,0:T(8,128)S(1)}, u32[]{:S(2)}, u32[]{:S(2)}) collective-permute-start(f32[65,8,128]{2,1,0:T(8,128)S(1)} %get-tuple-element.25), channel_id=1, source_target_pairs={{0,32},{16,48},{32,64},{48,80},{64,96},{80,112},{96,128},{112,144}... | collective-permute-start | bytes 798728 | tf_op jit(solution)/shard_map/ppermute | solution.py:217
  7.3 9.2 %collective-permute-start.3 = (f32[65,8,128]{2,1,0:T(8,128)S(1)}, f32[65,8,128]{2,1,0:T(8,128)S(1)}, u32[]{:S(2)}, u32[]{:S(2)}) collective-permute-start(f32[65,8,128]{2,1,0:T(8,128)S(1)} %get-tuple-element.26), channel_id=1, source_target_pairs={{0,240},{16,0},{32,16},{48,32},{64,48},{80,64},{96,80},{112,96},{1... | collective-permute-start | bytes 798728 | tf_op jit(solution)/shard_map/ppermute | solution.py:217
  16.9 5.4 %collective-permute-start.4 = (f32[5,8,128]{2,1,0:T(8,128)S(1)}, f32[5,8,128]{2,1,0:T(8,128)S(1)}, u32[]{:S(2)}, u32[]{:S(2)}) collective-permute-start(f32[5,8,128]{2,1,0:T(8,128)S(1)} %get-tuple-element.28), channel_id=1, source_target_pairs={{0,3},{1,2},{2,0},{3,1},{4,7},{5,6},{6,4},{7,5},{8,11},{9,10},{10,... | collective-permute-start | bytes 61448 | tf_op jit(solution)/shard_map/ppermute | solution.py:255
  20.0 5.0 %collective-permute-start.5 = (f32[5,8,128]{2,1,0:T(8,128)S(1)}, f32[5,8,128]{2,1,0:T(8,128)S(1)}, u32[]{:S(2)}, u32[]{:S(2)}) collective-permute-start(f32[5,8,128]{2,1,0:T(8,128)S(1)} %get-tuple-element.29), channel_id=1, source_target_pairs={{0,2},{1,3},{2,1},{3,0},{4,6},{5,7},{6,5},{7,4},{8,10},{9,11},{10,... | collective-permute-start | bytes 61448 | tf_op jit(solution)/shard_map/ppermute | solution.py:255
  20.5 4.5 %collective-permute-start.6 = (f32[5,8,128]{2,1,0:T(8,128)S(1)}, f32[5,8,128]{2,1,0:T(8,128)S(1)}, u32[]{:S(2)}, u32[]{:S(2)}) collective-permute-start(f32[5,8,128]{2,1,0:T(8,128)S(1)} %get-tuple-element.30), channel_id=1, source_target_pairs={{0,1},{1,0},{2,3},{3,2},{4,5},{5,4},{6,7},{7,6},{8,9},{9,8},{10,11... | collective-permute-start | bytes 61448 | tf_op jit(solution)/shard_map/ppermute | solution.py:255
